TPU v7x, 32 devices: a whole 2x2x4 slice. The times are simulated.
32 devices in a mesh: groups: 2 (over x), ctx: 8 (over z, y), head: 2 (over core).
Axes of the slice: x: 2, y: 2, z: 4, core: 2. Of those that a mesh axis runs over, the one named last changes fastest.
Arguments:
- query_rows: bfloat16 [4096, 2048], P(('groups', 'ctx'), 'head'), parts along dimension 0, may hold values from -6 to 6
- key_rows: bfloat16 [4096, 256], P(('groups', 'ctx'), 'head'), parts along dimension 0, may hold values from -6 to 6
- value_rows: bfloat16 [4096, 256], P(('groups', 'ctx'), 'head'), parts along dimension 0, may hold values from -6 to 6
- out_grad: bfloat16 [4096, 2048], P(('groups', 'ctx'), 'head'), parts along dimension 0, may hold values from -6 to 6
- doc_lengths: int32 [32], P('groups'), parts along dimension 0, may hold values from 1 to 256, 2048 in all
Outputs:
- attended: bfloat16 [4096, 2048], P(('groups', 'ctx'), 'head'), parts along dimension 0
- query_grad: bfloat16 [4096, 2048], P(('groups', 'ctx'), 'head'), parts along dimension 0
- key_grad: bfloat16 [4096, 256], P(('groups', 'ctx'), 'head'), parts along dimension 0
- value_grad: bfloat16 [4096, 256], P(('groups', 'ctx'), 'head'), parts along dimension 0
There are 2 independent parts, one for each index of `groups`. A program takes and returns all parts, laid end to end along the dimension named above; each array names one. Nothing has to cross between parts.
Inputs may be any that keep to these rules, and one draw needn't show every extreme that they name: `doc_lengths`: documents are laid end to end in position order and their lengths sum to 2048; the longest has exactly 256 tokens.
All inputs are finite; a program needn't handle non-finite values.
Results may differ from a plain program's by a relative error of at most 0.017.
Values may be sent and summed in bfloat16 or wider, within the bound.
A program may use at most 64 MiB of HBM per device.

v0:
```python
import jax
import jax.numpy as jnp
from jax import lax
from jax.sharding import PartitionSpec as P

HEAD_DIM = 128
DOC_STRETCHES = 8


def from_behind(value, axis, by):
    count = lax.axis_size(axis)
    pairs = [(i, i + by) for i in range(count) if 0 <= i + by < count]
    return lax.ppermute(value, axis, pairs)


def documents(positions, doc_lengths):
    starts = jnp.cumsum(doc_lengths) - doc_lengths
    return jnp.sum((starts[None, :] <= positions[:, None]).astype(jnp.int32), axis=1) - 1


def fetch_direct(packed, band_reach):
    blocks = []
    for offset in range(-band_reach, band_reach + 1):
        if offset == 0:
            blocks.append(packed)
        else:
            blocks.append(from_behind(packed, "ctx", -offset))
    return jnp.stack(blocks)


def return_direct(partials, band_reach):
    summed = partials[band_reach]
    for offset in range(-band_reach, band_reach + 1):
        if offset != 0:
            summed = summed + from_behind(
                partials[offset + band_reach].astype(jnp.bfloat16), "ctx", offset
            ).astype(jnp.float32)
    return summed


def shards(query_rows, key_rows, value_rows, out_grad, doc_lengths):
    ctx_count = lax.axis_size("ctx")
    my_index = lax.axis_index("ctx")
    tok_dev = query_rows.shape[0]
    stretch_len = tok_dev // 2
    kv_width = key_rows.shape[1]
    kv_local = kv_width // HEAD_DIM
    heads_local = query_rows.shape[1] // HEAD_DIM
    group_size = heads_local // kv_local
    scaling = HEAD_DIM ** (-0.5)
    band_reach = min(DOC_STRETCHES, ctx_count // 4)
    step_total = band_reach + 1
    step_list = jnp.arange(step_total, dtype=jnp.int32)
    inside = my_index + step_list <= ctx_count - 1
    fold_shift = 2 * ctx_count - 1 - 2 * my_index
    packed = jnp.concatenate([key_rows, value_rows], axis=1)
    kv_window = fetch_direct(packed, band_reach)
    low_window = kv_window[:, :stretch_len]
    low_keys = low_window[: band_reach + 1][::-1]
    upper_pick = kv_window[band_reach:, stretch_len:]
    blank = jnp.zeros((step_total,) + low_window.shape[1:], low_window.dtype)
    padded_rev = jnp.concatenate([blank, low_window[::-1], blank], axis=0)
    fold_pick = lax.dynamic_slice_in_dim(
        padded_rev, step_total + band_reach - fold_shift, step_total, 0
    )
    high_keys = jnp.where(inside[:, None, None], upper_pick, fold_pick)
    key_rows_all = jnp.stack([low_keys, high_keys]).reshape(
        2, step_total * stretch_len, 2 * kv_width
    )
    key_block = key_rows_all[..., :kv_width].reshape(2, -1, kv_local, HEAD_DIM)
    value_block = key_rows_all[..., kv_width:].reshape(2, -1, kv_local, HEAD_DIM)
    row_offsets = jnp.arange(stretch_len, dtype=jnp.int32)
    query_ids = jnp.stack([my_index, 2 * ctx_count - 1 - my_index])
    query_pos = query_ids[:, None] * stretch_len + row_offsets[None, :]
    key_ids = query_ids[:, None] - step_list[None, :]
    key_pos = (key_ids[:, :, None] * stretch_len + row_offsets[None, None, :]).reshape(2, -1)
    key_valid = jnp.broadcast_to((key_ids >= 0)[:, :, None], (2, step_total, stretch_len)).reshape(
        2, -1
    )
    query_doc = documents(query_pos.reshape(-1), doc_lengths).reshape(2, stretch_len)
    key_doc = documents(key_pos.reshape(-1), doc_lengths).reshape(2, -1)
    key_doc = jnp.where(key_valid, key_doc, -2)
    allowed = (key_doc[:, None, :] == query_doc[:, :, None]) & (
        key_pos[:, None, :] <= query_pos[:, :, None]
    )
    allowed = allowed[:, :, None, None, :]
    query_group = query_rows.reshape(2, stretch_len, kv_local, group_size, HEAD_DIM)
    grad_group = out_grad.reshape(2, stretch_len, kv_local, group_size, HEAD_DIM)
    scores = (
        jnp.einsum("sqgjd,skgd->sqgjk", query_group, key_block, preferred_element_type=jnp.float32)
        * scaling
    )
    masked = jnp.where(allowed, scores, -jnp.inf)
    row_top = jnp.max(masked, axis=-1)
    log_total = row_top + jnp.log(jnp.sum(jnp.exp(masked - row_top[..., None]), axis=-1))
    weights = jnp.exp(jnp.where(allowed, scores - log_total[..., None], -jnp.inf))
    weights_low = weights.astype(jnp.bfloat16)
    attended_group = jnp.einsum(
        "sqgjk,skgd->sqgjd", weights_low, value_block, preferred_element_type=jnp.float32
    ).astype(jnp.bfloat16)
    attended = attended_group.reshape(tok_dev, heads_local * HEAD_DIM)
    row_delta = jnp.sum(
        grad_group.astype(jnp.float32) * attended_group.astype(jnp.float32), axis=-1
    )
    weight_grad = jnp.einsum(
        "sqgjd,skgd->sqgjk", grad_group, value_block, preferred_element_type=jnp.float32
    )
    score_grad = (weights * (weight_grad - row_delta[..., None])).astype(jnp.bfloat16)
    query_grad = (
        (
            jnp.einsum(
                "sqgjk,skgd->sqgjd", score_grad, key_block, preferred_element_type=jnp.float32
            )
            * scaling
        )
        .astype(jnp.bfloat16)
        .reshape(tok_dev, heads_local * HEAD_DIM)
    )
    key_part = (
        jnp.einsum("sqgjk,sqgjd->skgd", score_grad, query_group, preferred_element_type=jnp.float32)
        * scaling
    )
    value_part = jnp.einsum(
        "sqgjk,sqgjd->skgd", weights_low, grad_group, preferred_element_type=jnp.float32
    )
    pieces = jnp.concatenate(
        [
            key_part.reshape(2, step_total, stretch_len, kv_width),
            value_part.reshape(2, step_total, stretch_len, kv_width),
        ],
        axis=-1,
    )
    inside_mask = inside[:, None, None]
    upper_piece = jnp.where(inside_mask, pieces[1], 0.0)
    folded_rev = jnp.where(inside_mask, 0.0, pieces[1])[::-1]
    gap = jnp.zeros((band_reach, stretch_len, 2 * kv_width), jnp.float32)
    margin = jnp.zeros((step_total, stretch_len, 2 * kv_width), jnp.float32)
    spread = jnp.concatenate(
        [margin, jnp.zeros((2 * band_reach + 1, stretch_len, 2 * kv_width), jnp.float32), margin],
        axis=0,
    )
    spread = lax.dynamic_update_slice_in_dim(spread, folded_rev, step_total + fold_shift, 0)
    folded_part = spread[step_total : step_total + 2 * band_reach + 1]
    lower_half = jnp.concatenate([pieces[0][::-1], gap], axis=0) + folded_part
    upper_half = jnp.concatenate([gap, upper_piece], axis=0)
    part_window = jnp.concatenate([lower_half, upper_half], axis=1)
    returned = return_direct(part_window, band_reach)
    key_grad = returned[:, :kv_width].astype(jnp.bfloat16)
    value_grad = returned[:, kv_width:].astype(jnp.bfloat16)
    return (attended, query_grad, key_grad, value_grad)


def solution(mesh):
    placed = (
        P(("groups", "ctx"), "head"),
        P(("groups", "ctx"), "head"),
        P(("groups", "ctx"), "head"),
        P(("groups", "ctx"), "head"),
        P("groups"),
    )
    return jax.shard_map(
        shards,
        mesh=mesh,
        in_specs=placed,
        out_specs=(
            P(("groups", "ctx"), "head"),
            P(("groups", "ctx"), "head"),
            P(("groups", "ctx"), "head"),
            P(("groups", "ctx"), "head"),
        ),
        check_vma=False,
    )
```

profile of v0, /device:TPU:20, one launch (start us, length us, event | category | flops | bytes accessed | tf_op | source)
XLA Modules:
  0.0 52.8 jit_solution(11190821810330131273)
XLA Ops:
  0.7 0.9 %constant_dynamic-update-slice_fusion.1 = bf16[256,256]{1,0:T(8,128)(2,1)S(1)} fusion(bf16[256,128]{1,0:T(8,128)(2,1)} %param.6), kind=kLoop, calls=%fused_computation.74 | loop fusion | bytes 131072
  1.6 0.9 %constant_dynamic-update-slice_fusion = bf16[256,256]{1,0:T(8,128)(2,1)S(1)} fusion(bf16[256,256]{1,0:T(8,128)(2,1)S(1)} %constant_dynamic-update-slice_fusion.1, bf16[256,128]{1,0:T(8,128)(2,1)} %param.7), kind=kLoop, calls=%fused_computation.73 | loop fusion | bytes 131072 | tf_op jit(solution)/shard_map/concatenate | solution.py:56
  2.5 3.5 %collective-permute-start = (bf16[256,256]{1,0:T(8,128)(2,1)S(1)}, bf16[256,256]{1,0:T(8,128)(2,1)S(1)}, u32[]{:S(2)}, u32[]{:S(2)}) collective-permute-start(bf16[256,256]{1,0:T(8,128)(2,1)S(1)} %constant_dynamic-update-slice_fusion), channel_id=1, source_target_pairs={{0,4},{2,6},{4,8},{6,10},{8,12},{10,14},{1,5},{3,7},{5,9},{7,11},{... | collective-permute-start | bytes 393224 | tf_op jit(solution)/shard_map/ppermute | solution.py:13
  5.9 1.9 %collective-permute-start.1 = (bf16[256,256]{1,0:T(8,128)(2,1)S(1)}, bf16[256,256]{1,0:T(8,128)(2,1)}, u32[]{:S(2)}, u32[]{:S(2)}) collective-permute-start(bf16[256,256]{1,0:T(8,128)(2,1)S(1)} %constant_dynamic-update-slice_fusion), channel_id=1, source_target_pairs={{0,2},{2,4},{4,6},{6,8},{8,10},{10,12},{12,14},{1,3},{3,5},{5,7},{... | collective-permute-start | bytes 393224 | tf_op jit(solution)/shard_map/ppermute | solution.py:13
  7.9 3.9 %collective-permute-start.2 = (bf16[256,256]{1,0:T(8,128)(2,1)S(1)}, bf16[256,256]{1,0:T(8,128)(2,1)}, u32[]{:S(2)}, u32[]{:S(2)}) collective-permute-start(bf16[256,256]{1,0:T(8,128)(2,1)S(1)} %constant_dynamic-update-slice_fusion), channel_id=1, source_target_pairs={{2,0},{4,2},{6,4},{8,6},{10,8},{12,10},{14,12},{3,1},{5,3},{7,5},{... | collective-permute-start | bytes 393224 | tf_op jit(solution)/shard_map/ppermute | solution.py:13
  11.8 2.4 %collective-permute-start.3 = (bf16[256,256]{1,0:T(8,128)(2,1)S(1)}, bf16[256,256]{1,0:T(8,128)(2,1)}, u32[]{:S(2)}, u32[]{:S(2)}) collective-permute-start(bf16[256,256]{1,0:T(8,128)(2,1)S(1)} %constant_dynamic-update-slice_fusion), channel_id=1, source_target_pairs={{4,0},{6,2},{8,4},{10,6},{12,8},{14,10},{5,1},{7,3},{9,5},{11,7},{... | collective-permute-start | bytes 393224 | tf_op jit(solution)/shard_map/ppermute | solution.py:13
  14.2 0.1 broadcast_multiply_fusion
  14.5 0.7 %copy.30 = s32[16,1]{1,0:T(8,128)S(1)} copy(s32[16,1]{0,1:T(1,128)} %bitcast.209) | data formatting | bytes 128 | tf_op jit(solution)/shard_map/reshape.246
  15.3 0.1 reduce.3
  15.4 0.7 %sub.78 = s32[16]{0:T(128)S(1)} subtract(s32[16]{0:T(128)S(1)} %reduce.3, s32[16]{0:T(128)} %param.9) | non-fusion elementwise | flops 16 | bytes 192 | tf_op jit(solution)/shard_map/sub | solution.py:17
  16.0 0.1 convert_reduce_fusion
  16.3 0.1 convert_reduce_fusion.1
  16.4 1.1 %convert_bitcast_fusion = f32[32,8,8,128]{3,1,2,0:T(8,128)S(1)} fusion(bf16[256,1024]{1,0:T(8,128)(2,1)} %param.8), kind=kLoop, calls=%fused_computation.25 | loop fusion | flops 262144 | bytes 1572864
  17.6 0.1 pad.5.clone
  17.7 1.3 %pad_maximum_fusion = f32[11,128,256]{2,1,0:T(8,128)} fusion(f32[3,128,256]{2,1,0:T(8,128)S(1)} %broadcast_in_dim.82, f32[11]{0:T(128)S(1)} %pad.5.clone), kind=kLoop, calls=%fused_computation.15 | loop fusion | flops 720896 | bytes 1835052 | tf_op jit(solution)/shard_map/concatenate | solution.py:138
  19.0 0.3 compare_and_fusion
  19.3 0.1 copy.56
  19.4 0.9 %copy.58 = bf16[32,8,8,128]{3,2,1,0:T(8,128)(2,1)} copy(bf16[32,8,8,128]{3,1,2,0:T(8,128)(2,1)S(1)} %bitcast.189) | data formatting | bytes 1048576
  20.3 0.2 copy.59
  20.5 1.3 %copy.36 = f32[2,128,1,8,128]{1,4,3,0,2:T(8,128)} copy(f32[2,128,1,8,128]{4,3,1,0,2:T(8,128)S(1)} %bitcast.186) | data formatting | bytes 2097152 | tf_op jit(solution)/shard_map/convert_element_type | solution.py:103
  21.8 0.9 %constant_dynamic-update-slice_fusion.5 = bf16[5,256,256]{2,1,0:T(8,128)(2,1)S(1)} fusion(bf16[5,256,256]{2,1,0:T(8,128)(2,1)S(1)} %constant_dynamic-update-slice_fusion.6, bf16[256,256]{1,0:T(8,128)(2,1)} %collective-permute-done.1), kind=kLoop, calls=%fused_computation.78 | loop fusion | bytes 262144
  22.8 0.9 %constant_dynamic-update-slice_fusion.3 = bf16[5,256,256]{2,1,0:T(8,128)(2,1)S(1)} fusion(bf16[5,256,256]{2,1,0:T(8,128)(2,1)S(1)} %constant_dynamic-update-slice_fusion.4, bf16[256,256]{1,0:T(8,128)(2,1)} %collective-permute-done.2), kind=kLoop, calls=%fused_computation.76 | loop fusion | bytes 262144
  23.7 0.9 %constant_dynamic-update-slice_fusion.2 = bf16[5,256,256]{2,1,0:T(8,128)(2,1)S(1)} fusion(bf16[5,256,256]{2,1,0:T(8,128)(2,1)S(1)} %constant_dynamic-update-slice_fusion.3, bf16[256,256]{1,0:T(8,128)(2,1)} %collective-permute-done.3), kind=kLoop, calls=%fused_computation.75 | loop fusion | bytes 262144 | tf_op jit(solution)/shard_map/stack | solution.py:28
  24.7 1.1 %fusion.42 = (bf16[3,128,256]{2,1,0:T(8,128)(2,1)S(1)}, bf16[3,128,256]{2,1,0:T(8,128)(2,1)S(1)}) fusion(s32[]{:T(128)S(6)} %select_n.33, bf16[3,128,256]{2,1,0:T(8,128)(2,1)S(1)} %broadcast_in_dim.49, bf16[5,128,256]{2,1,0:T(8,128)(2,1)S(1)} %rev.13, bf16[1,256,256]{2,1,0:T(8,128)(2,1)} %bitcast.5, bf16[1,256,256]{2,1,0:T(8,128)(2,1)} %bitcast.4, ...), kind=kLoop, calls=%fused_computation.57 | loop fusion | flops 1867776 | bytes 1572871 | tf_op jit(solution)/shard_map/jit(_where)/select_n | solution.py:66
  25.8 0.6 %fusion.3 = (f32[2,128,8]{1,2,0:T(8,128)S(1)}, f32[2,384,128,8]{2,1,3,0:T(8,128)S(1)}) fusion(pred[2,128,384]{1,2,0:T(8,128)(4,1)S(1)} %compare_and_fusion, bf16[2,128,8,128]{3,2,1,0:T(8,128)(2,1)S(1)} %bitcast.184, bf16[1,384,256]{2,1,0:T(8,128)(2,1)S(1)} %bitcast.196, bf16[1,384,256]{2,1,0:T(8,128)(2,1)S(1)} %bitcast.192), kind=kOutput, calls=%fused_computation.8 | convolution fusion | flops 204077056 | bytes 4169728 | tf_op jit(solution)/shard_map/sqgjd,skgd->sqgjk/dot_general | solution.py:90
  26.4 0.7 %exponential_reduce_fusion = f32[2,128,8]{1,2,0:T(8,128)S(1)} fusion(f32[2,384,128,8]{2,1,3,0:T(8,128)S(1)} %get-tuple-element.21, f32[2,128,8]{1,2,0:T(8,128)S(1)} %get-tuple-element.20, pred[2,128,384]{1,2,0:T(8,128)(4,1)S(1)} %compare_and_fusion), kind=kLoop, calls=%fused_computation.7 | loop fusion | flops 3143680 | bytes 3260416 | tf_op jit(solution)/shard_map/reduce_sum | solution.py:95
  27.1 0.8 %fusion.26 = f32[2,384,128,1]{2,1,3,0:T(8,128)S(1)} fusion(bf16[2,128,8,128]{3,2,1,0:T(8,128)(2,1)S(1)} %bitcast.204, f32[2,384,128,8]{2,1,3,0:T(8,128)S(1)} %get-tuple-element.21, f32[2,128,8]{1,2,0:T(8,128)S(1)} %log_add_fusion, pred[2,128,384]{1,2,0:T(8,128)(4,1)S(1)} %compare_and_fusion), kind=kOutput, calls=%fused_computation.35 | convolution fusion | flops 204472320 | bytes 4169728 | tf_op jit(solution)/shard_map/sqgjk,sqgjd->skgd/dot_general | solution.py:123
  28.0 0.3 copy-done.2
  28.3 1.7 %multiply_reduce_fusion = (f32[2,128,8]{1,2,0:T(8,128)S(1)}, bf16[2,128,1,8,128]{1,4,3,0,2:T(8,128)(2,1)}) fusion(f32[2,128,1,8,128]{1,4,3,0,2:T(8,128)S(1)} %copy-done.2, f32[2,384,128,8]{2,1,3,0:T(8,128)S(1)} %get-tuple-element.21, f32[2,128,8]{1,2,0:T(8,128)S(1)} %log_add_fusion, pred[2,128,384]{1,2,0:T(8,128)(4,1)S(1)} %compare_and_fusion, ...), kind=kOutput, calls=%fused_computation.26 | convolution fusion | flops 205912064 | bytes 5226496 | tf_op jit(solution)/shard_map/sqgjk,skgd->sqgjd/dot_general | solution.py:98
  30.1 1.1 %fusion = bf16[2,128,1,8,384]{1,4,3,0,2:T(8,128)(2,1)S(1)} fusion(f32[2,384,128,8]{2,1,3,0:T(8,128)S(1)} %get-tuple-element.21, f32[2,128,8]{1,2,0:T(8,128)S(1)} %get-tuple-element.22, f32[2,128,8]{1,2,0:T(8,128)S(1)} %log_add_fusion, pred[2,128,384]{1,2,0:T(8,128)(4,1)S(1)} %compare_and_fusion, bf16[2,128,8,128]{3,2,1,0:T(8,128)(2,1)S(1)} %bitcast.205, ...), kind=kOutput, calls=%fused_computation.1 | convolution fusion | flops 206438400 | bytes 5750784 | tf_op jit(solution)/shard_map/sqgjd,skgd->sqgjk/dot_general | solution.py:105
  31.2 0.6 %fusion.23 = f32[2,384,128]{2,1,0:T(8,128)S(1)} fusion(bf16[2,128,1,8,384]{1,4,3,0,2:T(8,128)(2,1)S(1)} %fusion, bf16[2,128,8,128]{3,2,1,0:T(8,128)(2,1)S(1)} %bitcast.185), kind=kOutput, calls=%fused_computation.24 | convolution fusion | flops 201424896 | bytes 2490368 | tf_op jit(solution)/shard_map/sqgjk,sqgjd->skgd/dot_general | solution.py:120
  31.8 0.9 %broadcast_select_fusion.1 = (f32[3,128,256]{2,1,0:T(8,128)}, f32[3,128,256]{2,1,0:T(8,128)S(1)}) fusion(pred[3]{0:T(512)(128)(4,1)S(1)} %add_compare_fusion, f32[2,3,128,128]{3,2,1,0:T(8,128)S(1)} %bitcast.201, f32[2,3,128,128]{3,2,1,0:T(8,128)S(1)} %bitcast.188), kind=kLoop, calls=%fused_computation.67 | loop fusion | flops 294912 | bytes 1572867 | tf_op jit(solution)/shard_map/jit(_where)/select_n | solution.py:135
  32.7 0.5 fusion.17
  33.3 1.0 %reverse_dynamic-update-slice_fusion = f32[11,128,256]{2,1,0:T(8,128)S(1)} fusion(f32[11,128,256]{2,1,0:T(8,128)S(1)} %copy-done, s32[]{:T(128)S(6)} %select_n.39, f32[3,128,256]{2,1,0:T(8,128)} %get-tuple-element.6), kind=kLoop, calls=%fused_computation.47 | loop fusion | bytes 786436 | tf_op jit(solution)/shard_map/dynamic_update_slice | solution.py:142
  34.3 0.1 slice_add_fusion
  34.5 0.8 %slice_bitcast_fusion.4 = (bf16[256,256]{1,0:T(8,128)(2,1)}, bf16[256,256]{1,0:T(8,128)(2,1)}, bf16[256,256]{1,0:T(8,128)(2,1)}, bf16[256,256]{1,0:T(8,128)(2,1)}) fusion(bf16[5,256,256]{2,1,0:T(8,128)(2,1)S(1)} %fusion.59), kind=kLoop, calls=%fused_computation.71 | loop fusion | bytes 1048576 | tf_op jit(solution)/shard_map/convert_element_type | solution.py:36
  35.3 3.0 %collective-permute-start.4 = (bf16[256,256]{1,0:T(8,128)(2,1)}, bf16[256,256]{1,0:T(8,128)(2,1)S(1)}, u32[]{:S(2)}, u32[]{:S(2)}) collective-permute-start(bf16[256,256]{1,0:T(8,128)(2,1)} %get-tuple-element.8), channel_id=1, source_target_pairs={{4,0},{6,2},{8,4},{10,6},{12,8},{14,10},{5,1},{7,3},{9,5},{11,7},{... | collective-permute-start | bytes 393224 | tf_op jit(solution)/shard_map/ppermute | solution.py:13
  38.3 2.2 %collective-permute-start.5 = (bf16[256,256]{1,0:T(8,128)(2,1)}, bf16[256,256]{1,0:T(8,128)(2,1)S(1)}, u32[]{:S(2)}, u32[]{:S(2)}) collective-permute-start(bf16[256,256]{1,0:T(8,128)(2,1)} %get-tuple-element.11), channel_id=1, source_target_pairs={{2,0},{4,2},{6,4},{8,6},{10,8},{12,10},{14,12},{3,1},{5,3},{7,5},{... | collective-permute-start | bytes 393224 | tf_op jit(solution)/shard_map/ppermute | solution.py:13
  40.5 4.5 %collective-permute-start.6 = (bf16[256,256]{1,0:T(8,128)(2,1)}, bf16[256,256]{1,0:T(8,128)(2,1)S(1)}, u32[]{:S(2)}, u32[]{:S(2)}) collective-permute-start(bf16[256,256]{1,0:T(8,128)(2,1)} %get-tuple-element.10), channel_id=1, source_target_pairs={{0,2},{2,4},{4,6},{6,8},{8,10},{10,12},{12,14},{1,3},{3,5},{5,7},{... | collective-permute-start | bytes 393224 | tf_op jit(solution)/shard_map/ppermute | solution.py:13
  45.0 1.9 %collective-permute-start.7 = (bf16[256,256]{1,0:T(8,128)(2,1)}, bf16[256,256]{1,0:T(8,128)(2,1)S(1)}, u32[]{:S(2)}, u32[]{:S(2)}) collective-permute-start(bf16[256,256]{1,0:T(8,128)(2,1)} %get-tuple-element.9), channel_id=1, source_target_pairs={{0,4},{2,6},{4,8},{6,10},{8,12},{10,14},{1,5},{3,7},{5,9},{7,11},{... | collective-permute-start | bytes 393224 | tf_op jit(solution)/shard_map/ppermute | solution.py:13
  46.9 0.3 copy.39
  47.2 0.9 %copy.75 = bf16[32,8,8,128]{3,1,2,0:T(8,128)(2,1)} copy(bf16[32,8,8,128]{3,2,1,0:T(8,128)(2,1)S(1)} %bitcast.190) | data formatting | bytes 1048576
  48.1 0.3 copy.34
  48.5 0.9 %copy.76 = bf16[32,8,8,128]{3,1,2,0:T(8,128)(2,1)} copy(bf16[32,8,8,128]{3,2,1,0:T(8,128)(2,1)S(1)} %bitcast.191) | data formatting | bytes 1048576
  49.4 0.1 select_maximum_fusion
  49.5 2.6 %collective-permute-done.7 = bf16[256,256]{1,0:T(8,128)(2,1)S(1)} collective-permute-done((bf16[256,256]{1,0:T(8,128)(2,1)}, bf16[256,256]{1,0:T(8,128)(2,1)S(1)}, u32[]{:S(2)}, u32[]{:S(2)}) %collective-permute-start.7) | collective-permute-done | bytes 131104 | tf_op jit(solution)/shard_map/ppermute | solution.py:13
  52.1 0.1 fusion.39
  52.2 0.7 %fusion.60 = (bf16[256,128]{1,0:T(8,128)(2,1)}, bf16[256,128]{1,0:T(8,128)(2,1)}) fusion(bf16[256,256]{1,0:T(8,128)(2,1)S(1)} %fusion.39), kind=kLoop, calls=%fused_computation.103 | loop fusion | bytes 262144 | tf_op jit(solution)/shard_map/slice | solution.py:149
  (43 shorter events, 0.8 us)
Async XLA Ops:
  0.6 18.8 %copy-start.1 = (bf16[256,1024]{1,0:T(8,128)(2,1)S(1)}, bf16[256,1024]{1,0:T(8,128)(2,1)}, u32[]{:S(2)}) copy-start(bf16[256,1024]{1,0:T(8,128)(2,1)} %param.8) | copy-start | bytes 1572868
  0.6 18.6 %copy-start.3 = (bf16[256,1024]{1,0:T(8,128)(2,1)S(1)}, bf16[256,1024]{1,0:T(8,128)(2,1)}, u32[]{:S(2)}) copy-start(bf16[256,1024]{1,0:T(8,128)(2,1)} %param.5) | copy-start | bytes 1572868
  2.5 19.4 %collective-permute-start = (bf16[256,256]{1,0:T(8,128)(2,1)S(1)}, bf16[256,256]{1,0:T(8,128)(2,1)S(1)}, u32[]{:S(2)}, u32[]{:S(2)}) collective-permute-start(bf16[256,256]{1,0:T(8,128)(2,1)S(1)} %constant_dynamic-update-slice_fusion), channel_id=1, source_target_pairs={{0,4},{2,6},{4,8},{6,10},{8,12},{10,14},{1,5},{3,7},{5,9},{7,11},{... | collective-permute-start | bytes 393224 | tf_op jit(solution)/shard_map/ppermute | solution.py:13
  5.9 15.9 %collective-permute-start.1 = (bf16[256,256]{1,0:T(8,128)(2,1)S(1)}, bf16[256,256]{1,0:T(8,128)(2,1)}, u32[]{:S(2)}, u32[]{:S(2)}) collective-permute-start(bf16[256,256]{1,0:T(8,128)(2,1)S(1)} %constant_dynamic-update-slice_fusion), channel_id=1, source_target_pairs={{0,2},{2,4},{4,6},{6,8},{8,10},{10,12},{12,14},{1,3},{3,5},{5,7},{... | collective-permute-start | bytes 393224 | tf_op jit(solution)/shard_map/ppermute | solution.py:13
  7.9 14.9 %collective-permute-start.2 = (bf16[256,256]{1,0:T(8,128)(2,1)S(1)}, bf16[256,256]{1,0:T(8,128)(2,1)}, u32[]{:S(2)}, u32[]{:S(2)}) collective-permute-start(bf16[256,256]{1,0:T(8,128)(2,1)S(1)} %constant_dynamic-update-slice_fusion), channel_id=1, source_target_pairs={{2,0},{4,2},{6,4},{8,6},{10,8},{12,10},{14,12},{3,1},{5,3},{7,5},{... | collective-permute-start | bytes 393224 | tf_op jit(solution)/shard_map/ppermute | solution.py:13
  11.8 11.9 %collective-permute-start.3 = (bf16[256,256]{1,0:T(8,128)(2,1)S(1)}, bf16[256,256]{1,0:T(8,128)(2,1)}, u32[]{:S(2)}, u32[]{:S(2)}) collective-permute-start(bf16[256,256]{1,0:T(8,128)(2,1)S(1)} %constant_dynamic-update-slice_fusion), channel_id=1, source_target_pairs={{4,0},{6,2},{8,4},{10,6},{12,8},{14,10},{5,1},{7,3},{9,5},{11,7},{... | collective-permute-start | bytes 393224 | tf_op jit(solution)/shard_map/ppermute | solution.py:13
  25.8 1.3 %copy-start.4 = (bf16[32,8,8,128]{3,2,1,0:T(8,128)(2,1)S(1)}, bf16[32,8,8,128]{3,2,1,0:T(8,128)(2,1)}, u32[]{:S(2)}) copy-start(bf16[32,8,8,128]{3,2,1,0:T(8,128)(2,1)} %copy.58) | copy-start | bytes 1572868
  27.1 1.2 %copy-start.2 = (f32[2,128,1,8,128]{1,4,3,0,2:T(8,128)S(1)}, f32[2,128,1,8,128]{1,4,3,0,2:T(8,128)}, u32[]{:S(2)}) copy-start(f32[2,128,1,8,128]{1,4,3,0,2:T(8,128)} %copy.36) | copy-start | bytes 3145732
  31.8 1.5 %copy-start = (f32[11,128,256]{2,1,0:T(8,128)S(1)}, f32[11,128,256]{2,1,0:T(8,128)}, u32[]{:S(2)}) copy-start(f32[11,128,256]{2,1,0:T(8,128)} %pad_maximum_fusion) | copy-start | bytes 4325380
  34.4 13.7 %copy-start.5 = (bf16[2,128,1,8,128]{1,4,3,0,2:T(8,128)(2,1)S(1)}, bf16[2,128,1,8,128]{1,4,3,0,2:T(8,128)(2,1)}, u32[]{:S(2)}) copy-start(bf16[2,128,1,8,128]{1,4,3,0,2:T(8,128)(2,1)} %get-tuple-element.23) | copy-start | bytes 1572868
  35.3 14.2 %collective-permute-start.4 = (bf16[256,256]{1,0:T(8,128)(2,1)}, bf16[256,256]{1,0:T(8,128)(2,1)S(1)}, u32[]{:S(2)}, u32[]{:S(2)}) collective-permute-start(bf16[256,256]{1,0:T(8,128)(2,1)} %get-tuple-element.8), channel_id=1, source_target_pairs={{4,0},{6,2},{8,4},{10,6},{12,8},{14,10},{5,1},{7,3},{9,5},{11,7},{... | collective-permute-start | bytes 393224 | tf_op jit(solution)/shard_map/ppermute | solution.py:13
  38.3 11.2 %collective-permute-start.5 = (bf16[256,256]{1,0:T(8,128)(2,1)}, bf16[256,256]{1,0:T(8,128)(2,1)S(1)}, u32[]{:S(2)}, u32[]{:S(2)}) collective-permute-start(bf16[256,256]{1,0:T(8,128)(2,1)} %get-tuple-element.11), channel_id=1, source_target_pairs={{2,0},{4,2},{6,4},{8,6},{10,8},{12,10},{14,12},{3,1},{5,3},{7,5},{... | collective-permute-start | bytes 393224 | tf_op jit(solution)/shard_map/ppermute | solution.py:13
  40.5 9.0 %collective-permute-start.6 = (bf16[256,256]{1,0:T(8,128)(2,1)}, bf16[256,256]{1,0:T(8,128)(2,1)S(1)}, u32[]{:S(2)}, u32[]{:S(2)}) collective-permute-start(bf16[256,256]{1,0:T(8,128)(2,1)} %get-tuple-element.10), channel_id=1, source_target_pairs={{0,2},{2,4},{4,6},{6,8},{8,10},{10,12},{12,14},{1,3},{3,5},{5,7},{... | collective-permute-start | bytes 393224 | tf_op jit(solution)/shard_map/ppermute | solution.py:13
  45.0 7.1 %collective-permute-start.7 = (bf16[256,256]{1,0:T(8,128)(2,1)}, bf16[256,256]{1,0:T(8,128)(2,1)S(1)}, u32[]{:S(2)}, u32[]{:S(2)}) collective-permute-start(bf16[256,256]{1,0:T(8,128)(2,1)} %get-tuple-element.9), channel_id=1, source_target_pairs={{0,4},{2,6},{4,8},{6,10},{8,12},{10,14},{1,5},{3,7},{5,9},{7,11},{... | collective-permute-start | bytes 393224 | tf_op jit(solution)/shard_map/ppermute | solution.py:13
where the time goes:
time: 53.5 us; the launch traced here: 52.8 us
  starting transfers between devices  23.3 us (44%)
  local copies, waits for them, and re-layouts  13.4 us (25%)
  other arithmetic  7.09 us (13%)
  matrix products  5.35 us (10%)
  waiting for transfers between devices  2.6 us (5%)
  between operations  1.07 us (2%)
    ppermute x8, starting transfers between devices, from_behind(): return lax.ppermute(value, axis, pairs)  23.3 us
    unnamed x23, local copies, waits for them, and re-layouts  6.25 us
    ppermute x8, waiting for transfers between devices, from_behind(): return lax.ppermute(value, axis, pairs)  2.6 us
    dot_general x1, matrix products, shards(): jnp.einsum('sqgjk,skgd->sqgjd', weights_low, value_block, preferred_eleme...  1.74 us
    convert_element_type x1, local copies, waits for them, and re-layouts, shards(): grad_group.astype(jnp.float32) * attended_group.astype(jnp.float32)  1.32 us
    concatenate x1, other arithmetic, shards(): jnp.concatenate([margin, jnp.zeros((2 * band_reach + 1, stretch_len, 2 *...  1.31 us
    unnamed x1, other arithmetic  1.15 us
    dot_general x1, matrix products, shards(): jnp.einsum('sqgjd,skgd->sqgjk', grad_group, value_block, preferred_elemen...  1.11 us
  transfers between devices with their start and end apart: 8, of which 1 were waited for; matrix products, arithmetic and copies ran while one was open for 23% of the time, Pallas kernels for 0%

commit v1 on v0

v1 whole, which is shorter than its diff:
```python
import functools
import math

import jax
import jax.numpy as jnp
from jax import lax
from jax.experimental import pallas as pl
from jax.experimental.pallas import tpu as pltpu
from jax.sharding import PartitionSpec as P

HEAD_DIM = 128
DOC_STRETCHES = 8
PAIR = 2
MESH = pl.DeviceIdType.MESH
NT = (((1,), (1,)), ((), ()))


def kernel(
    n,
    reach,
    heads,
    docs_ref,
    q_hbm,
    k_hbm,
    v_hbm,
    g_hbm,
    att_ref,
    dq_ref,
    dk_ref,
    dv_ref,
    q_buf,
    g_buf,
    k_buf,
    v_buf,
    s_own,
    w_own,
    p_buf,
    d_buf,
    part_out,
    part_in,
    load_sem,
    kv_send,
    kv_recv,
    part_send,
    part_recv,
):
    st = q_hbm.shape[0] // 2
    me = lax.axis_index("ctx")
    last = 2 * n - 1
    scaling = HEAD_DIM**-0.5
    wide = PAIR * HEAD_DIM
    rows = [slice(half * st, (half + 1) * st) for half in range(2)]
    dot = functools.partial(lax.dot_general, preferred_element_type=jnp.float32)

    def matmul(a, b):
        return dot(a, b, (((1,), (0,)), ((), ())))

    loads = []
    for half in range(2):
        for slot, (src, dst) in enumerate(
            (
                (k_hbm, k_buf.at[half, 0]),
                (q_hbm, q_buf.at[half]),
                (v_hbm, v_buf.at[half, 0]),
                (g_hbm, g_buf.at[half]),
            )
        ):
            copy = pltpu.make_async_copy(src.at[rows[half]], dst, load_sem.at[half, slot])
            copy.start()
            loads.append(copy)

    barrier = pltpu.get_barrier_semaphore()
    for by in range(1, reach + 1):
        for sign in (-1, 1):
            other = me + sign * by

            @pl.when((other >= 0) & (other < n))
            def _():
                pl.semaphore_signal(
                    barrier, inc=1, device_id={"ctx": other}, device_id_type=MESH
                )

    for d in range(1, reach + 1):

        @pl.when(me < d)
        def _():
            k_buf[0, d] = jnp.zeros_like(k_buf[0, d])
            v_buf[0, d] = jnp.zeros_like(v_buf[0, d])
            part_in[1, d - 1] = jnp.zeros_like(part_in[1, d - 1])

    pl.semaphore_wait(barrier, jnp.minimum(me, reach) + jnp.minimum(n - 1 - me, reach))

    def kv_copies(half, d, target, to_half):
        return [
            pltpu.make_async_remote_copy(
                src_ref=src.at[rows[half]],
                dst_ref=dst.at[to_half, d],
                send_sem=kv_send.at[half, d - 1, which],
                recv_sem=kv_recv.at[to_half, d - 1, which],
                device_id={"ctx": target},
                device_id_type=MESH,
            )
            for which, (src, dst) in enumerate(((k_hbm, k_buf), (v_hbm, v_buf)))
        ]

    def kv_routes(act):
        for d in range(1, reach + 1):
            up = me + d
            fold = last - up

            @pl.when(up < n)
            def _():
                for copy in kv_copies(0, d, up, 0):
                    act(copy)

            @pl.when((up >= n) & (fold != me))
            def _():
                for copy in kv_copies(0, d, fold, 1):
                    act(copy)

            @pl.when(me >= d)
            def _():
                for copy in kv_copies(1, d, me - d, 1):
                    act(copy)

    kv_routes(lambda copy: copy.start())

    lane = lax.broadcasted_iota(jnp.int32, (st, st), 1)
    sub = lax.broadcasted_iota(jnp.int32, (st, st), 0)
    lower = sub <= lane
    lower_low = lower.astype(jnp.float32).astype(jnp.bfloat16)
    lower_wide = jnp.concatenate([lower] * PAIR, axis=1)
    lower_low = jnp.concatenate([lower_low] * PAIR, axis=1)
    bias = []
    for half in range(2):
        stretch = me if half == 0 else last - me
        base = stretch * st
        row_pos = base + lane[:8]
        first = jnp.zeros((8, st), jnp.int32)
        begin = jnp.int32(0)
        for i in range(docs_ref.shape[0]):
            first = jnp.where(row_pos >= begin, begin, first)
            begin = begin + docs_ref[i]
        first = first[:1] - base
        blocks = [jnp.where(lower, sub, sub - reach * st)]
        blocks += [sub - d * st for d in range(1, reach)]
        blocks = [jnp.where(block >= first, 0.0, -1e30) for block in blocks]
        bias.append([jnp.concatenate([block] * PAIR, axis=1) for block in blocks])

    def gather(buf, half, first, count):
        cols = [
            buf[half, :, h * HEAD_DIM : (h + 1) * HEAD_DIM] for h in range(first, first + count)
        ]
        return jnp.concatenate(cols, axis=0)

    for copy in loads:
        copy.wait()

    for d in range(1, reach + 1):

        @pl.when(last - me - d == me)
        def _():
            k_buf[1, d] = k_buf[0, 0]
            v_buf[1, d] = v_buf[0, 0]

    for half in range(2):
        for h in range(0, heads, PAIR):
            cols = slice(h * HEAD_DIM, h * HEAD_DIM + wide)
            s_own[half, :, cols] = dot(k_buf[half, 0], gather(q_buf, half, h, PAIR), NT)
            w_own[half, :, cols] = dot(v_buf[half, 0], gather(g_buf, half, h, PAIR), NT)

    def part_copy(half, d, target, to_half):
        return pltpu.make_async_remote_copy(
            src_ref=part_out.at[half, d - 1],
            dst_ref=part_in.at[to_half, d - 1],
            send_sem=part_send.at[half, d - 1],
            recv_sem=part_recv.at[to_half, d - 1],
            device_id={"ctx": target},
            device_id_type=MESH,
        )

    def part_routes(half, d, act):
        if half == 0:

            @pl.when(me >= d)
            def _():
                act(part_copy(0, d, me - d, 0))

        else:
            up = me + d
            fold = last - up

            @pl.when(up < n)
            def _():
                act(part_copy(1, d, up, 1))

            @pl.when((up >= n) & (fold != me))
            def _():
                act(part_copy(1, d, fold, 0))

    def wait_kv(half, d):
        for copy in kv_copies(half, d, me, half):
            copy.wait_recv()

    for half in range(2):
        for d in range(1, reach + 1):
            arrives = (me >= d) if half == 0 else (last - me - d != me)

            @pl.when(arrives)
            def _():
                wait_kv(half, d)

        for h in range(0, heads, PAIR):
            cols = slice(h * HEAD_DIM, h * HEAD_DIM + wide)
            q_cols = gather(q_buf, half, h, PAIR)
            g_cols = gather(g_buf, half, h, PAIR)
            far = dot(k_buf[half, reach], q_cols, NT)
            scores = [jnp.where(lower_wide, s_own[half, :, cols], far)]
            scores += [dot(k_buf[half, d], q_cols, NT) for d in range(1, reach)]
            scores = [score + mask for score, mask in zip(scores, bias[half])]
            top = functools.reduce(jnp.maximum, scores)
            top = jnp.max(top, axis=0, keepdims=True)
            factor = scaling * math.log2(math.e)
            weights = [jnp.exp2((score - top) * factor) for score in scores]
            total = jnp.sum(functools.reduce(jnp.add, weights), axis=0, keepdims=True)
            inverse = 1.0 / total
            weights = [weight * inverse for weight in weights]
            far = dot(v_buf[half, reach], g_cols, NT)
            grads = [jnp.where(lower_wide, w_own[half, :, cols], far)]
            grads += [dot(v_buf[half, d], g_cols, NT) for d in range(1, reach)]
            delta = functools.reduce(jnp.add, [w * g for w, g in zip(weights, grads)])
            delta = jnp.sum(delta, axis=0, keepdims=True)
            for d in range(reach):
                low = weights[d].astype(jnp.bfloat16)
                slope = (weights[d] * (grads[d] - delta)).astype(jnp.bfloat16)
                if d == 0:
                    low_own = low * lower_low
                    slope_own = slope * lower_low
                    p_buf[half, :st, cols] = low_own
                    d_buf[half, :st, cols] = slope_own
                    p_buf[half, reach * st :, cols] = low - low_own
                    d_buf[half, reach * st :, cols] = slope - slope_own
                else:
                    p_buf[half, d * st : (d + 1) * st, cols] = low
                    d_buf[half, d * st : (d + 1) * st, cols] = slope

        part_out[half, :, :st] = (
            (matmul(d_buf[half, st:], gather(q_buf, half, 0, heads)) * scaling)
            .astype(jnp.bfloat16)
            .reshape(reach, st, HEAD_DIM)
        )
        part_out[half, :, st:] = (
            matmul(p_buf[half, st:], gather(g_buf, half, 0, heads))
            .astype(jnp.bfloat16)
            .reshape(reach, st, HEAD_DIM)
        )
        for d in range(1, reach + 1):
            part_routes(half, d, lambda copy: copy.start())

    for d in range(1, reach + 1):

        @pl.when(last - me - d == me)
        def _():
            part_in[0, d - 1] = part_out[1, d - 1]

    for half in range(2):
        k_turn = jnp.concatenate([k_buf[half, d].T for d in range(reach + 1)], axis=1)
        v_turn = jnp.concatenate([v_buf[half, d].T for d in range(reach + 1)], axis=1)
        for h in range(0, heads, PAIR):
            cols = slice(h * HEAD_DIM, h * HEAD_DIM + wide)
            att = matmul(v_turn, p_buf[half, :, cols])
            grad = matmul(k_turn, d_buf[half, :, cols]) * scaling
            for j in range(PAIR):
                own = slice(j * HEAD_DIM, (j + 1) * HEAD_DIM)
                out = slice((h + j) * HEAD_DIM, (h + j + 1) * HEAD_DIM)
                att_ref[rows[half], out] = att[:, own].T.astype(jnp.bfloat16)
                dq_ref[rows[half], out] = grad[:, own].T.astype(jnp.bfloat16)

    for half in range(2):
        key_own = matmul(d_buf[half, :st], gather(q_buf, half, 0, heads)) * scaling
        value_own = matmul(p_buf[half, :st], gather(g_buf, half, 0, heads))
        for d in range(1, reach + 1):
            arrives = (last - me - d != me) if half == 0 else (me >= d)

            @pl.when(arrives)
            def _():
                part_copy(half, d, me, half).wait_recv()

        for d in range(reach):
            key_own += part_in[half, d, :st].astype(jnp.float32)
            value_own += part_in[half, d, st:].astype(jnp.float32)
        dk_ref[rows[half]] = key_own.astype(jnp.bfloat16)
        dv_ref[rows[half]] = value_own.astype(jnp.bfloat16)

    kv_routes(lambda copy: copy.wait_send())
    for half in range(2):
        for d in range(1, reach + 1):
            part_routes(half, d, lambda copy: copy.wait_send())


def shards(query_rows, key_rows, value_rows, out_grad, doc_lengths):
    n = lax.axis_size("ctx")
    reach = min(DOC_STRETCHES, n // 4)
    tok, width = query_rows.shape
    st = tok // 2
    heads = width // HEAD_DIM
    low = jnp.bfloat16
    vmem = pl.BlockSpec(memory_space=pltpu.VMEM)
    hbm = pl.BlockSpec(memory_space=pl.ANY)
    like = lambda x: jax.ShapeDtypeStruct(x.shape, low)
    macs = 2 * heads * st * st * (reach + 1) * HEAD_DIM * 6
    return pl.pallas_call(
        functools.partial(kernel, n, reach, heads),
        out_shape=(like(query_rows), like(query_rows), like(key_rows), like(key_rows)),
        in_specs=[pl.BlockSpec(memory_space=pltpu.SMEM), hbm, hbm, hbm, hbm],
        out_specs=(vmem,) * 4,
        scratch_shapes=[
            pltpu.VMEM((2, st, width), low),
            pltpu.VMEM((2, st, width), low),
            pltpu.VMEM((2, reach + 1, st, HEAD_DIM), low),
            pltpu.VMEM((2, reach + 1, st, HEAD_DIM), low),
            pltpu.VMEM((2, st, width), jnp.float32),
            pltpu.VMEM((2, st, width), jnp.float32),
            pltpu.VMEM((2, (reach + 1) * st, width), low),
            pltpu.VMEM((2, (reach + 1) * st, width), low),
            pltpu.VMEM((2, reach, 2 * st, HEAD_DIM), low),
            pltpu.VMEM((2, reach, 2 * st, HEAD_DIM), low),
            pltpu.SemaphoreType.DMA((2, 4)),
            pltpu.SemaphoreType.DMA((2, reach, 2)),
            pltpu.SemaphoreType.DMA((2, reach, 2)),
            pltpu.SemaphoreType.DMA((2, reach)),
            pltpu.SemaphoreType.DMA((2, reach)),
        ],
        compiler_params=pltpu.CompilerParams(
            collective_id=0, has_side_effects=True, vmem_limit_bytes=40 * 1024 * 1024
        ),
        cost_estimate=pl.CostEstimate(
            flops=2 * macs,
            bytes_accessed=8 * tok * width + 8 * tok * HEAD_DIM,
            transcendentals=2 * heads * st * st * reach,
        ),
    )(doc_lengths, query_rows, key_rows, value_rows, out_grad)


def solution(mesh):
    rows = P(("groups", "ctx"), "head")
    return jax.shard_map(
        shards,
        mesh=mesh,
        in_specs=(rows, rows, rows, rows, P("groups")),
        out_specs=(rows,) * 4,
        check_vma=False,
    )
```

time: 53.5 us -> 22.8 us (0.43)
  the two profiles are of different devices: /device:TPU:20 before, /device:TPU:0 now
where the time goes in v1:
time: 22.8 us; the launch traced here: 22.4 us
  Pallas kernels  14.5 us (64%)
  local copies, waits for them, and re-layouts  7.25 us (32%)
  between operations  0.65 us (3%)
    pallas_call x1, Pallas kernels, shards(): pl.pallas_call(functools.partial(kernel, n, reach, heads), out_shape=(lik...  14.5 us
    unnamed x14, local copies, waits for them, and re-layouts  7.25 us

profile of v1, /device:TPU:0, one launch (start us, length us, event | category | flops | bytes accessed | tf_op | source)
XLA Modules:
  0.0 22.4 jit_solution(2216668522842226497)
XLA Ops:
  0.6 0.0 copy-start
  0.6 1.0 %copy-done = bf16[256,1024]{1,0:T(8,128)(2,1)S(1)} copy-done((bf16[256,1024]{1,0:T(8,128)(2,1)S(1)}, bf16[256,1024]{1,0:T(8,128)(2,1)}, u32[]{:S(2)}) %copy-start) | copy-done | bytes 524312
  1.7 0.0 copy-start.1
  1.7 1.0 %copy-done.1 = bf16[256,1024]{1,0:T(8,128)(2,1)S(1)} copy-done((bf16[256,1024]{1,0:T(8,128)(2,1)S(1)}, bf16[256,1024]{1,0:T(8,128)(2,1)}, u32[]{:S(2)}) %copy-start.1) | copy-done | bytes 524312
  2.7 0.0 copy-start.2
  2.7 0.8 %copy-done.2 = bf16[256,128]{1,0:T(8,128)(2,1)S(1)} copy-done((bf16[256,128]{1,0:T(8,128)(2,1)S(1)}, bf16[256,128]{1,0:T(8,128)(2,1)}, u32[]{:S(2)}) %copy-start.2) | copy-done | bytes 65560
  3.6 0.0 copy-start.3
  3.6 0.8 %copy-done.3 = bf16[256,128]{1,0:T(8,128)(2,1)S(1)} copy-done((bf16[256,128]{1,0:T(8,128)(2,1)S(1)}, bf16[256,128]{1,0:T(8,128)(2,1)}, u32[]{:S(2)}) %copy-start.3) | copy-done | bytes 65560
  4.4 0.0 copy-start.4
  4.4 0.7 %copy-done.4 = s32[16]{0:T(128)S(1)} copy-done((s32[16]{0:T(128)S(1)}, s32[16]{0:T(128)}, u32[]{:S(2)}) %copy-start.4) | copy-done | bytes 88
  5.1 14.5 %shard_map.84 = (bf16[256,1024]{1,0:T(8,128)(2,1)S(1)}, bf16[256,1024]{1,0:T(8,128)(2,1)S(1)}, bf16[256,128]{1,0:T(8,128)(2,1)S(1)}, bf16[256,128]{1,0:T(8,128)(2,1)S(1)}) custom-call(s32[16]{0:T(128)S(1)} %copy-done.4, bf16[256,1024]{1,0:T(8,128)(2,1)S(1)} %copy-done, bf16[256,128]{1,0:T(8,128)(2,1)S(1)} %copy-done.2, bf16[256,128]{1,0:T(8,128)(2,1)S(1)} %copy-done.3, ...), custom_call_target="tpu_custom_call" | custom-call | flops 1207959552 | bytes 2359296 | tf_op jit(solution)/shard_map/pallas_call | solution.py:312
  19.6 0.8 %copy.13 = bf16[256,1024]{1,0:T(8,128)(2,1)} copy(bf16[256,1024]{1,0:T(8,128)(2,1)S(1)} %get-tuple-element.8) | data formatting | bytes 1048576
  20.4 0.8 %copy.14 = bf16[256,1024]{1,0:T(8,128)(2,1)} copy(bf16[256,1024]{1,0:T(8,128)(2,1)S(1)} %get-tuple-element.9) | data formatting | bytes 1048576
  21.2 0.6 %copy.15 = bf16[256,128]{1,0:T(8,128)(2,1)} copy(bf16[256,128]{1,0:T(8,128)(2,1)S(1)} %get-tuple-element.10) | data formatting | bytes 131072
  21.8 0.6 %copy.16 = bf16[256,128]{1,0:T(8,128)(2,1)} copy(bf16[256,128]{1,0:T(8,128)(2,1)S(1)} %get-tuple-element.11) | data formatting | bytes 131072
Async XLA Ops:
  0.6 1.0 %copy-start = (bf16[256,1024]{1,0:T(8,128)(2,1)S(1)}, bf16[256,1024]{1,0:T(8,128)(2,1)}, u32[]{:S(2)}) copy-start(bf16[256,1024]{1,0:T(8,128)(2,1)} %q_hbm.1) | copy-start | bytes 1572868
  1.7 1.0 %copy-start.1 = (bf16[256,1024]{1,0:T(8,128)(2,1)S(1)}, bf16[256,1024]{1,0:T(8,128)(2,1)}, u32[]{:S(2)}) copy-start(bf16[256,1024]{1,0:T(8,128)(2,1)} %g_hbm.1) | copy-start | bytes 1572868
  2.7 0.8 %copy-start.2 = (bf16[256,128]{1,0:T(8,128)(2,1)S(1)}, bf16[256,128]{1,0:T(8,128)(2,1)}, u32[]{:S(2)}) copy-start(bf16[256,128]{1,0:T(8,128)(2,1)} %k_hbm.1) | copy-start | bytes 196612
  3.6 0.8 %copy-start.3 = (bf16[256,128]{1,0:T(8,128)(2,1)S(1)}, bf16[256,128]{1,0:T(8,128)(2,1)}, u32[]{:S(2)}) copy-start(bf16[256,128]{1,0:T(8,128)(2,1)} %v_hbm.1) | copy-start | bytes 196612
  4.4 0.7 %copy-start.4 = (s32[16]{0:T(128)S(1)}, s32[16]{0:T(128)}, u32[]{:S(2)}) copy-start(s32[16]{0:T(128)} %docs_ref.1) | copy-start | bytes 196

commit v2 on v1

--- a/solution.py
+++ b/solution.py
@@ -19,7 +19,7 @@
     n,
     reach,
     heads,
-    docs_ref,
+    docs_hbm,
     q_hbm,
     k_hbm,
     v_hbm,
@@ -28,6 +28,7 @@
     dq_ref,
     dk_ref,
     dv_ref,
+    docs_ref,
     q_buf,
     g_buf,
     k_buf,
@@ -38,6 +39,7 @@
     d_buf,
     part_out,
     part_in,
+    docs_sem,
     load_sem,
     kv_send,
     kv_recv,
@@ -55,6 +57,8 @@
     def matmul(a, b):
         return dot(a, b, (((1,), (0,)), ((), ())))
 
+    docs_copy = pltpu.make_async_copy(docs_hbm, docs_ref, docs_sem)
+    docs_copy.start()
     loads = []
     for half in range(2):
         for slot, (src, dst) in enumerate(
@@ -124,6 +128,8 @@
                     act(copy)
 
     kv_routes(lambda copy: copy.start())
+
+    docs_copy.wait()
 
     lane = lax.broadcasted_iota(jnp.int32, (st, st), 1)
     sub = lax.broadcasted_iota(jnp.int32, (st, st), 0)
@@ -298,6 +304,15 @@
             part_routes(half, d, lambda copy: copy.wait_send())
 
 
+def write_out(*refs):
+    sems = refs[8]
+    copies = [pltpu.make_async_copy(refs[i], refs[4 + i], sems.at[i]) for i in range(4)]
+    for copy in copies:
+        copy.start()
+    for copy in copies:
+        copy.wait()
+
+
 def shards(query_rows, key_rows, value_rows, out_grad, doc_lengths):
     n = lax.axis_size("ctx")
     reach = min(DOC_STRETCHES, n // 4)
@@ -306,15 +321,18 @@
     heads = width // HEAD_DIM
     low = jnp.bfloat16
     vmem = pl.BlockSpec(memory_space=pltpu.VMEM)
-    hbm = pl.BlockSpec(memory_space=pl.ANY)
+    hbm = pl.BlockSpec(memory_space=pltpu.HBM)
+    anywhere = pl.BlockSpec(memory_space=pl.ANY)
     like = lambda x: jax.ShapeDtypeStruct(x.shape, low)
     macs = 2 * heads * st * st * (reach + 1) * HEAD_DIM * 6
-    return pl.pallas_call(
+    shapes = (like(query_rows), like(query_rows), like(key_rows), like(key_rows))
+    results = pl.pallas_call(
         functools.partial(kernel, n, reach, heads),
-        out_shape=(like(query_rows), like(query_rows), like(key_rows), like(key_rows)),
-        in_specs=[pl.BlockSpec(memory_space=pltpu.SMEM), hbm, hbm, hbm, hbm],
+        out_shape=shapes,
+        in_specs=[hbm, hbm, hbm, hbm, hbm],
         out_specs=(vmem,) * 4,
         scratch_shapes=[
+            pltpu.SMEM(doc_lengths.shape, jnp.int32),
             pltpu.VMEM((2, st, width), low),
             pltpu.VMEM((2, st, width), low),
             pltpu.VMEM((2, reach + 1, st, HEAD_DIM), low),
@@ -325,6 +343,7 @@
             pltpu.VMEM((2, (reach + 1) * st, width), low),
             pltpu.VMEM((2, reach, 2 * st, HEAD_DIM), low),
             pltpu.VMEM((2, reach, 2 * st, HEAD_DIM), low),
+            pltpu.SemaphoreType.DMA,
             pltpu.SemaphoreType.DMA((2, 4)),
             pltpu.SemaphoreType.DMA((2, reach, 2)),
             pltpu.SemaphoreType.DMA((2, reach, 2)),
@@ -339,7 +358,17 @@
             bytes_accessed=8 * tok * width + 8 * tok * HEAD_DIM,
             transcendentals=2 * heads * st * st * reach,
         ),
-    )(doc_lengths, query_rows, key_rows, value_rows, out_grad)
+    )(*[
+        pltpu.with_memory_space_constraint(x, pltpu.HBM)
+        for x in (doc_lengths, query_rows, key_rows, value_rows, out_grad)
+    ])
+    return pl.pallas_call(
+        write_out,
+        out_shape=shapes,
+        in_specs=[anywhere] * 4,
+        out_specs=(hbm,) * 4,
+        scratch_shapes=[pltpu.SemaphoreType.DMA((4,))],
+    )(*results)
 
 
 def solution(mesh):

time: 22.8 us -> 54.5 us (2.39)
  Pallas kernels: 14.5 us -> 50.9 us
  local copies, waits for them, and re-layouts: 7.25 us -> 2.83 us
    pallas_call x1 -> x2, Pallas kernels: 14.5 us -> 50.9 us  [the longest x1 36.9 us: shards(): pl.pallas_call(write_out, out_shape=shapes, in_specs=[anywhere] * 4, out_...]
    unnamed x14 -> x8, local copies, waits for them, and re-layouts: 7.25 us -> 2.83 us
where the time goes in v2:
time: 54.5 us; the launch traced here: 54.3 us
  Pallas kernels  50.9 us (93%)
  local copies, waits for them, and re-layouts  2.83 us (5%)
  between operations  0.65 us (1%)
    pallas_call x1, Pallas kernels, shards(): pl.pallas_call(write_out, out_shape=shapes, in_specs=[anywhere] * 4, out_...  36.9 us
    pallas_call x1, Pallas kernels, shards(): pl.pallas_call(functools.partial(kernel, n, reach, heads), out_shape=shap...  14 us
    unnamed x8, local copies, waits for them, and re-layouts  2.83 us

profile of v2, /device:TPU:0, one launch (start us, length us, event | category | flops | bytes accessed | tf_op | source)
XLA Modules:
  0.0 54.3 jit_solution(11190238499113543995)
XLA Ops:
  0.6 14.0 %shard_map.84 = (bf16[256,1024]{1,0:T(8,128)(2,1)S(1)}, bf16[256,1024]{1,0:T(8,128)(2,1)S(1)}, bf16[256,128]{1,0:T(8,128)(2,1)S(1)}, bf16[256,128]{1,0:T(8,128)(2,1)S(1)}) custom-call(s32[16]{0:T(128)} %docs_hbm.1, bf16[256,1024]{1,0:T(8,128)(2,1)} %q_hbm.1, bf16[256,128]{1,0:T(8,128)(2,1)} %k_hbm.1, bf16[256,128]{1,0:T(8,128)(2,1)} %v_hbm.1, ...), custom_call_target="tpu_custom_call" | custom-call | flops 1207959552 | bytes 2359296 | tf_op jit(solution)/shard_map/pallas_call | solution.py:329
  14.6 0.0 copy-start
  14.6 0.8 %copy-done = bf16[256,1024]{1,0:T(8,128)(2,1)} copy-done((bf16[256,1024]{1,0:T(8,128)(2,1)}, bf16[256,1024]{1,0:T(8,128)(2,1)S(1)}, u32[]{:S(2)}) %copy-start) | copy-done | bytes 524312
  15.4 0.0 copy-start.1
  15.4 0.8 %copy-done.1 = bf16[256,1024]{1,0:T(8,128)(2,1)} copy-done((bf16[256,1024]{1,0:T(8,128)(2,1)}, bf16[256,1024]{1,0:T(8,128)(2,1)S(1)}, u32[]{:S(2)}) %copy-start.1) | copy-done | bytes 524312
  16.2 0.0 copy-start.2
  16.2 0.6 %copy-done.2 = bf16[256,128]{1,0:T(8,128)(2,1)} copy-done((bf16[256,128]{1,0:T(8,128)(2,1)}, bf16[256,128]{1,0:T(8,128)(2,1)S(1)}, u32[]{:S(2)}) %copy-start.2) | copy-done | bytes 65560
  16.8 0.0 copy-start.3
  16.8 0.6 %copy-done.3 = bf16[256,128]{1,0:T(8,128)(2,1)} copy-done((bf16[256,128]{1,0:T(8,128)(2,1)}, bf16[256,128]{1,0:T(8,128)(2,1)S(1)}, u32[]{:S(2)}) %copy-start.3) | copy-done | bytes 65560
  17.5 36.9 %shard_map.85 = (bf16[256,1024]{1,0:T(8,128)(2,1)}, bf16[256,1024]{1,0:T(8,128)(2,1)}, bf16[256,128]{1,0:T(8,128)(2,1)}, bf16[256,128]{1,0:T(8,128)(2,1)}) custom-call(bf16[256,1024]{1,0:T(8,128)(2,1)} %copy-done, bf16[256,1024]{1,0:T(8,128)(2,1)} %copy-done.1, bf16[256,128]{1,0:T(8,128)(2,1)} %copy-done.2, bf16[256,128]{1,0:T(8,128)(2,1)} %copy-done.3), custom_call_target="tpu_custom_call" | custom-call | tf_op jit(solution)/shard_map/pallas_call | solution.py:365
Async XLA Ops:
  14.6 0.8 %copy-start = (bf16[256,1024]{1,0:T(8,128)(2,1)}, bf16[256,1024]{1,0:T(8,128)(2,1)S(1)}, u32[]{:S(2)}) copy-start(bf16[256,1024]{1,0:T(8,128)(2,1)S(1)} %get-tuple-element.8.refs_0_) | copy-start | bytes 1572868
  15.4 0.8 %copy-start.1 = (bf16[256,1024]{1,0:T(8,128)(2,1)}, bf16[256,1024]{1,0:T(8,128)(2,1)S(1)}, u32[]{:S(2)}) copy-start(bf16[256,1024]{1,0:T(8,128)(2,1)S(1)} %get-tuple-element.9.refs_1_) | copy-start | bytes 1572868
  16.2 0.6 %copy-start.2 = (bf16[256,128]{1,0:T(8,128)(2,1)}, bf16[256,128]{1,0:T(8,128)(2,1)S(1)}, u32[]{:S(2)}) copy-start(bf16[256,128]{1,0:T(8,128)(2,1)S(1)} %get-tuple-element.10.refs_2_) | copy-start | bytes 196612
  16.8 0.6 %copy-start.3 = (bf16[256,128]{1,0:T(8,128)(2,1)}, bf16[256,128]{1,0:T(8,128)(2,1)S(1)}, u32[]{:S(2)}) copy-start(bf16[256,128]{1,0:T(8,128)(2,1)S(1)} %get-tuple-element.11.refs_3_) | copy-start | bytes 196612

commit v3 on v2

v3 whole, which is shorter than its diff:
```python
import functools
import math

import jax
import jax.numpy as jnp
from jax import lax
from jax.experimental import pallas as pl
from jax.experimental.pallas import tpu as pltpu
from jax.sharding import PartitionSpec as P

HEAD_DIM = 128
DOC_STRETCHES = 8
PAIR = 2
MESH = pl.DeviceIdType.MESH
NT = (((1,), (1,)), ((), ()))


def kernel(
    n,
    reach,
    heads,
    docs_hbm,
    q_hbm,
    k_hbm,
    v_hbm,
    g_hbm,
    att_ref,
    dq_ref,
    dk_ref,
    dv_ref,
    docs_ref,
    q_buf,
    g_buf,
    k_buf,
    v_buf,
    s_own,
    w_own,
    w_buf,
    p_buf,
    d_buf,
    part_out,
    part_in,
    docs_sem,
    load_sem,
    kv_send,
    kv_recv,
    part_send,
    part_recv,
):
    st = q_hbm.shape[0] // 2
    me = lax.axis_index("ctx")
    last = 2 * n - 1
    scaling = HEAD_DIM**-0.5
    wide = PAIR * HEAD_DIM
    rows = [slice(half * st, (half + 1) * st) for half in range(2)]
    dot = functools.partial(lax.dot_general, preferred_element_type=jnp.float32)

    def matmul(a, b):
        return dot(a, b, (((1,), (0,)), ((), ())))

    barrier = pltpu.get_barrier_semaphore()
    for by in range(1, reach + 1):
        for sign in (-1, 1):
            other = me + sign * by

            @pl.when((other >= 0) & (other < n))
            def _():
                pl.semaphore_signal(
                    barrier, inc=1, device_id={"ctx": other}, device_id_type=MESH
                )

    docs_copy = pltpu.make_async_copy(docs_hbm, docs_ref, docs_sem)
    docs_copy.start()
    loads = []
    for half in range(2):
        for slot, (src, dst) in enumerate(
            (
                (k_hbm, k_buf.at[half, 0]),
                (q_hbm, q_buf.at[half]),
                (v_hbm, v_buf.at[half, 0]),
                (g_hbm, g_buf.at[half]),
            )
        ):
            copy = pltpu.make_async_copy(src.at[rows[half]], dst, load_sem.at[half, slot])
            copy.start()
            loads.append(copy)

    for d in range(1, reach + 1):

        @pl.when(me < d)
        def _():
            k_buf[0, d] = jnp.zeros_like(k_buf[0, d])
            v_buf[0, d] = jnp.zeros_like(v_buf[0, d])
            part_in[:, 1, d - 1] = jnp.zeros_like(part_in[:, 1, d - 1])

        @pl.when((me + d >= n) & (last - me - d > me))
        def _():
            part_in[:, 0, d - 1] = jnp.zeros_like(part_in[:, 0, d - 1])

    docs_copy.wait()

    lane = lax.broadcasted_iota(jnp.int32, (st, st), 1)
    sub = lax.broadcasted_iota(jnp.int32, (st, st), 0)
    lower = sub <= lane
    lower_low = lower.astype(jnp.float32).astype(jnp.bfloat16)
    lower_wide = jnp.concatenate([lower] * PAIR, axis=1)
    lower_low = jnp.concatenate([lower_low] * PAIR, axis=1)
    bias = []
    for half in range(2):
        stretch = me if half == 0 else last - me
        base = stretch * st
        row_pos = base + lane[:8]
        first = jnp.zeros((8, st), jnp.int32)
        begin = jnp.int32(0)
        for i in range(docs_ref.shape[0]):
            first = jnp.where(row_pos >= begin, begin, first)
            begin = begin + docs_ref[i]
        first = first[:1] - base
        blocks = [jnp.where(lower, sub, sub - reach * st)]
        blocks += [sub - d * st for d in range(1, reach)]
        blocks = [jnp.where(block >= first, 0.0, -1e30) for block in blocks]
        bias.append([jnp.concatenate([block] * PAIR, axis=1) for block in blocks])

    pl.semaphore_wait(barrier, jnp.minimum(me, reach) + jnp.minimum(n - 1 - me, reach))

    def kv_copy(which, half, d, target, to_half):
        src, dst = ((k_hbm, k_buf), (v_hbm, v_buf))[which]
        return pltpu.make_async_remote_copy(
            src_ref=src.at[rows[half]],
            dst_ref=dst.at[to_half, d],
            send_sem=kv_send.at[half, d - 1, which],
            recv_sem=kv_recv.at[to_half, d - 1, which],
            device_id={"ctx": target},
            device_id_type=MESH,
        )

    def kv_routes(which, act):
        for d in range(1, reach + 1):
            up = me + d
            fold = last - up

            @pl.when(me >= d)
            def _():
                act(kv_copy(which, 1, d, me - d, 1))

            @pl.when(up < n)
            def _():
                act(kv_copy(which, 0, d, up, 0))

            @pl.when((up >= n) & (fold < me))
            def _():
                act(kv_copy(which, 0, d, fold, 1))

    def kv_arrive(which):
        buf = (k_buf, v_buf)[which]
        for d in range(1, reach + 1):

            @pl.when(me >= d)
            def _():
                kv_copy(which, 0, d, me, 0).wait_recv()

        for d in range(1, reach + 1):
            source = last - me - d

            @pl.when(source > me)
            def _():
                kv_copy(which, 1, d, me, 1).wait_recv()

            @pl.when(source <= me)
            def _():
                buf[1, d] = buf[0, me - source]

    kv_routes(0, lambda copy: copy.start())
    kv_routes(1, lambda copy: copy.start())

    def gather(buf, half, first, count):
        cols = [
            buf[half, :, h * HEAD_DIM : (h + 1) * HEAD_DIM] for h in range(first, first + count)
        ]
        return jnp.concatenate(cols, axis=0)

    for copy in loads:
        copy.wait()

    for half in (1, 0):
        for h in range(0, heads, PAIR):
            cols = slice(h * HEAD_DIM, h * HEAD_DIM + wide)
            s_own[half, :, cols] = dot(k_buf[half, 0], gather(q_buf, half, h, PAIR), NT)
            w_own[half, :, cols] = dot(v_buf[half, 0], gather(g_buf, half, h, PAIR), NT)

    def part_copy(which, half, d, target, to_half):
        return pltpu.make_async_remote_copy(
            src_ref=part_out.at[which, half, d - 1],
            dst_ref=part_in.at[which, to_half, d - 1],
            send_sem=part_send.at[which, half, d - 1],
            recv_sem=part_recv.at[which, to_half, d - 1],
            device_id={"ctx": target},
            device_id_type=MESH,
        )

    def part_routes(which, half, act):
        for d in range(1, reach + 1):
            up = me + d
            fold = last - up
            if half == 0:

                @pl.when(me >= d)
                def _():
                    act(part_copy(which, 0, d, me - d, 0))

            else:

                @pl.when(up < n)
                def _():
                    act(part_copy(which, 1, d, up, 1))

                @pl.when((up >= n) & (fold > me))
                def _():
                    act(part_copy(which, 1, d, fold, 0))

    def give_back(which, half, parts):
        part_out[which, half] = parts.astype(jnp.bfloat16).reshape(reach, st, HEAD_DIM)
        for d in range(1, reach + 1):
            if half == 0:
                twin = last - 2 * me + d

                @pl.when(twin <= reach)
                def _():
                    both = part_out[which, 0, d - 1].astype(jnp.float32)
                    both += part_out[which, 1, twin - 1].astype(jnp.float32)
                    part_out[which, 0, d - 1] = both.astype(jnp.bfloat16)

            else:

                @pl.when(last - me - d == me)
                def _():
                    part_in[which, 0, d - 1] = part_out[which, 1, d - 1]

        part_routes(which, half, lambda copy: copy.start())

    kv_arrive(0)
    factor = scaling * math.log2(math.e)
    for half in (1, 0):
        for h in range(0, heads, PAIR):
            cols = slice(h * HEAD_DIM, h * HEAD_DIM + wide)
            q_cols = gather(q_buf, half, h, PAIR)
            far = dot(k_buf[half, reach], q_cols, NT)
            scores = [jnp.where(lower_wide, s_own[half, :, cols], far)]
            scores += [dot(k_buf[half, d], q_cols, NT) for d in range(1, reach)]
            scores = [score + mask for score, mask in zip(scores, bias[half])]
            top = functools.reduce(jnp.maximum, scores)
            top = jnp.max(top, axis=0, keepdims=True)
            weights = [jnp.exp2((score - top) * factor) for score in scores]
            total = jnp.sum(functools.reduce(jnp.add, weights), axis=0, keepdims=True)
            inverse = 1.0 / total
            for d in range(reach):
                weight = weights[d] * inverse
                w_buf[half, d, :, cols] = weight
                low = weight.astype(jnp.bfloat16)
                if d == 0:
                    low_own = low * lower_low
                    p_buf[half, :st, cols] = low_own
                    p_buf[half, reach * st :, cols] = low - low_own
                else:
                    p_buf[half, d * st : (d + 1) * st, cols] = low
        give_back(1, half, matmul(p_buf[half, st:], gather(g_buf, half, 0, heads)))

    kv_arrive(1)
    for half in (1, 0):
        for h in range(0, heads, PAIR):
            cols = slice(h * HEAD_DIM, h * HEAD_DIM + wide)
            g_cols = gather(g_buf, half, h, PAIR)
            far = dot(v_buf[half, reach], g_cols, NT)
            grads = [jnp.where(lower_wide, w_own[half, :, cols], far)]
            grads += [dot(v_buf[half, d], g_cols, NT) for d in range(1, reach)]
            weights = [w_buf[half, d, :, cols] for d in range(reach)]
            delta = functools.reduce(jnp.add, [w * g for w, g in zip(weights, grads)])
            delta = jnp.sum(delta, axis=0, keepdims=True)
            for d in range(reach):
                slope = (weights[d] * (grads[d] - delta)).astype(jnp.bfloat16)
                if d == 0:
                    slope_own = slope * lower_low
                    d_buf[half, :st, cols] = slope_own
                    d_buf[half, reach * st :, cols] = slope - slope_own
                else:
                    d_buf[half, d * st : (d + 1) * st, cols] = slope
        give_back(0, half, matmul(d_buf[half, st:], gather(q_buf, half, 0, heads)) * scaling)

    for half in (1, 0):
        k_turn = jnp.concatenate([k_buf[half, d].T for d in range(reach + 1)], axis=1)
        v_turn = jnp.concatenate([v_buf[half, d].T for d in range(reach + 1)], axis=1)
        for h in range(0, heads, PAIR):
            cols = slice(h * HEAD_DIM, h * HEAD_DIM + wide)
            att = matmul(v_turn, p_buf[half, :, cols])
            grad = matmul(k_turn, d_buf[half, :, cols]) * scaling
            for j in range(PAIR):
                own = slice(j * HEAD_DIM, (j + 1) * HEAD_DIM)
                out = slice((h + j) * HEAD_DIM, (h + j + 1) * HEAD_DIM)
                att_ref[rows[half], out] = att[:, own].T.astype(jnp.bfloat16)
                dq_ref[rows[half], out] = grad[:, own].T.astype(jnp.bfloat16)

    for which, half in ((1, 1), (1, 0), (0, 1), (0, 0)):
        if which == 0:
            own = matmul(d_buf[half, :st], gather(q_buf, half, 0, heads)) * scaling
        else:
            own = matmul(p_buf[half, :st], gather(g_buf, half, 0, heads))
        for d in range(1, reach + 1):
            arrives = ((me + d < n) | (last - me - d < me)) if half == 0 else (me >= d)

            @pl.when(arrives)
            def _():
                part_copy(which, half, d, me, half).wait_recv()

        for d in range(reach):
            own += part_in[which, half, d].astype(jnp.float32)
        (dk_ref, dv_ref)[which][rows[half]] = own.astype(jnp.bfloat16)

    for which in range(2):
        kv_routes(which, lambda copy: copy.wait_send())
        for half in range(2):
            part_routes(which, half, lambda copy: copy.wait_send())


def write_out(*refs):
    sems = refs[8]
    copies = [pltpu.make_async_copy(refs[i], refs[4 + i], sems.at[i]) for i in range(4)]
    for copy in copies:
        copy.start()
    for copy in copies:
        copy.wait()


def shards(query_rows, key_rows, value_rows, out_grad, doc_lengths):
    n = lax.axis_size("ctx")
    reach = min(DOC_STRETCHES, n // 4)
    tok, width = query_rows.shape
    st = tok // 2
    heads = width // HEAD_DIM
    low = jnp.bfloat16
    vmem = pl.BlockSpec(memory_space=pltpu.VMEM)
    hbm = pl.BlockSpec(memory_space=pltpu.HBM)
    anywhere = pl.BlockSpec(memory_space=pl.ANY)
    like = lambda x: jax.ShapeDtypeStruct(x.shape, low)
    macs = 2 * heads * st * st * (reach + 1) * HEAD_DIM * 6
    shapes = (like(query_rows), like(query_rows), like(key_rows), like(key_rows))
    results = pl.pallas_call(
        functools.partial(kernel, n, reach, heads),
        out_shape=shapes,
        in_specs=[hbm, hbm, hbm, hbm, hbm],
        out_specs=(vmem,) * 4,
        scratch_shapes=[
            pltpu.SMEM(doc_lengths.shape, jnp.int32),
            pltpu.VMEM((2, st, width), low),
            pltpu.VMEM((2, st, width), low),
            pltpu.VMEM((2, reach + 1, st, HEAD_DIM), low),
            pltpu.VMEM((2, reach + 1, st, HEAD_DIM), low),
            pltpu.VMEM((2, st, width), jnp.float32),
            pltpu.VMEM((2, st, width), jnp.float32),
            pltpu.VMEM((2, reach, st, width), jnp.float32),
            pltpu.VMEM((2, (reach + 1) * st, width), low),
            pltpu.VMEM((2, (reach + 1) * st, width), low),
            pltpu.VMEM((2, 2, reach, st, HEAD_DIM), low),
            pltpu.VMEM((2, 2, reach, st, HEAD_DIM), low),
            pltpu.SemaphoreType.DMA,
            pltpu.SemaphoreType.DMA((2, 4)),
            pltpu.SemaphoreType.DMA((2, reach, 2)),
            pltpu.SemaphoreType.DMA((2, reach, 2)),
            pltpu.SemaphoreType.DMA((2, 2, reach)),
            pltpu.SemaphoreType.DMA((2, 2, reach)),
        ],
        compiler_params=pltpu.CompilerParams(
            collective_id=0, has_side_effects=True, vmem_limit_bytes=40 * 1024 * 1024
        ),
        cost_estimate=pl.CostEstimate(
            flops=2 * macs,
            bytes_accessed=8 * tok * width + 8 * tok * HEAD_DIM,
            transcendentals=2 * heads * st * st * reach,
        ),
    )(*[
        pltpu.with_memory_space_constraint(x, pltpu.HBM)
        for x in (doc_lengths, query_rows, key_rows, value_rows, out_grad)
    ])
    return pl.pallas_call(
        write_out,
        out_shape=shapes,
        in_specs=[anywhere] * 4,
        out_specs=(hbm,) * 4,
        scratch_shapes=[pltpu.SemaphoreType.DMA((4,))],
        compiler_params=pltpu.CompilerParams(vmem_limit_bytes=4 * 1024 * 1024),
    )(*results)


def solution(mesh):
    rows = P(("groups", "ctx"), "head")
    return jax.shard_map(
        shards,
        mesh=mesh,
        in_specs=(rows, rows, rows, rows, P("groups")),
        out_specs=(rows,) * 4,
        check_vma=False,
    )
```

time: 54.5 us -> 17 us (0.31)
  Pallas kernels: 50.9 us -> 16.2 us
  local copies, waits for them, and re-layouts: 2.83 us -> 0 us
    pallas_call x1, Pallas kernels: 36.9 us -> 1.03 us  [shards(): pl.pallas_call(write_out, out_shape=shapes, in_specs=[anywhere] * 4, out_...]
    unnamed x8 -> x0, local copies, waits for them, and re-layouts: 2.83 us -> none
    pallas_call x1, Pallas kernels: 14 us -> 15.1 us  [shards(): pl.pallas_call(functools.partial(kernel, n, reach, heads), out_shape=shap...]
where the time goes in v3:
time: 17 us; the launch traced here: 16.8 us
  Pallas kernels  16.2 us (95%)
  between operations  0.64 us (4%)
    pallas_call x1, Pallas kernels, shards(): pl.pallas_call(functools.partial(kernel, n, reach, heads), out_shape=shap...  15.1 us
    pallas_call x1, Pallas kernels, shards(): pl.pallas_call(write_out, out_shape=shapes, in_specs=[anywhere] * 4, out_...  1.03 us

profile of v3, /device:TPU:0, one launch (start us, length us, event | category | flops | bytes accessed | tf_op | source)
XLA Modules:
  0.0 16.8 jit_solution(15966596526118989311)
XLA Ops:
  0.6 15.1 %shard_map.84 = (bf16[256,1024]{1,0:T(8,128)(2,1)S(1)}, bf16[256,1024]{1,0:T(8,128)(2,1)S(1)}, bf16[256,128]{1,0:T(8,128)(2,1)S(1)}, bf16[256,128]{1,0:T(8,128)(2,1)S(1)}) custom-call(s32[16]{0:T(128)} %docs_hbm.1, bf16[256,1024]{1,0:T(8,128)(2,1)} %q_hbm.1, bf16[256,128]{1,0:T(8,128)(2,1)} %k_hbm.1, bf16[256,128]{1,0:T(8,128)(2,1)} %v_hbm.1, ...), custom_call_target="tpu_custom_call" | custom-call | flops 1207959552 | bytes 2359296 | tf_op jit(solution)/shard_map/pallas_call | solution.py:346
  15.8 1.0 %shard_map.85 = (bf16[256,1024]{1,0:T(8,128)(2,1)}, bf16[256,1024]{1,0:T(8,128)(2,1)}, bf16[256,128]{1,0:T(8,128)(2,1)}, bf16[256,128]{1,0:T(8,128)(2,1)}) custom-call(bf16[256,1024]{1,0:T(8,128)(2,1)S(1)} %get-tuple-element.8.refs_0_, bf16[256,1024]{1,0:T(8,128)(2,1)S(1)} %get-tuple-element.9.refs_1_, bf16[256,128]{1,0:T(8,128)(2,1)S(1)} %get-tuple-element.10.refs_2_, ...), custom_call_target="tpu_custom_call" | custom-call | tf_op jit(solution)/shard_map/pallas_call | solution.py:383

commit v4 on v3

--- a/solution.py
+++ b/solution.py
@@ -35,7 +35,6 @@
     v_buf,
     s_own,
     w_own,
-    w_buf,
     p_buf,
     d_buf,
     part_out,
@@ -91,11 +90,11 @@
         def _():
             k_buf[0, d] = jnp.zeros_like(k_buf[0, d])
             v_buf[0, d] = jnp.zeros_like(v_buf[0, d])
-            part_in[:, 1, d - 1] = jnp.zeros_like(part_in[:, 1, d - 1])
+            part_in[1, d - 1] = jnp.zeros_like(part_in[1, d - 1])
 
         @pl.when((me + d >= n) & (last - me - d > me))
         def _():
-            part_in[:, 0, d - 1] = jnp.zeros_like(part_in[:, 0, d - 1])
+            part_in[0, d - 1] = jnp.zeros_like(part_in[0, d - 1])
 
     docs_copy.wait()
 
@@ -134,44 +133,39 @@
             device_id_type=MESH,
         )
 
-    def kv_routes(which, act):
+    def kv_routes(half, act):
         for d in range(1, reach + 1):
             up = me + d
             fold = last - up
-
-            @pl.when(me >= d)
-            def _():
-                act(kv_copy(which, 1, d, me - d, 1))
-
-            @pl.when(up < n)
-            def _():
-                act(kv_copy(which, 0, d, up, 0))
-
-            @pl.when((up >= n) & (fold < me))
-            def _():
-                act(kv_copy(which, 0, d, fold, 1))
-
-    def kv_arrive(which):
-        buf = (k_buf, v_buf)[which]
-        for d in range(1, reach + 1):
-
-            @pl.when(me >= d)
-            def _():
-                kv_copy(which, 0, d, me, 0).wait_recv()
-
+            for which in range(2):
+                if half == 1:
+
+                    @pl.when(me >= d)
+                    def _():
+                        act(kv_copy(which, 1, d, me - d, 1))
+
+                else:
+
+                    @pl.when(up < n)
+                    def _():
+                        act(kv_copy(which, 0, d, up, 0))
+
+                    @pl.when((up >= n) & (fold < me))
+                    def _():
+                        act(kv_copy(which, 0, d, fold, 1))
+
+    def kv_arrive(half):
         for d in range(1, reach + 1):
             source = last - me - d
-
-            @pl.when(source > me)
-            def _():
-                kv_copy(which, 1, d, me, 1).wait_recv()
-
-            @pl.when(source <= me)
-            def _():
-                buf[1, d] = buf[0, me - source]
-
-    kv_routes(0, lambda copy: copy.start())
-    kv_routes(1, lambda copy: copy.start())
+            for which in range(2):
+                arrives = (me >= d) if half == 0 else (source > me)
+
+                @pl.when(arrives)
+                def _():
+                    kv_copy(which, half, d, me, half).wait_recv()
+
+    for half in (1, 0):
+        kv_routes(half, lambda copy: copy.start())
 
     def gather(buf, half, first, count):
         cols = [
@@ -188,17 +182,17 @@
             s_own[half, :, cols] = dot(k_buf[half, 0], gather(q_buf, half, h, PAIR), NT)
             w_own[half, :, cols] = dot(v_buf[half, 0], gather(g_buf, half, h, PAIR), NT)
 
-    def part_copy(which, half, d, target, to_half):
+    def part_copy(half, d, target, to_half):
         return pltpu.make_async_remote_copy(
-            src_ref=part_out.at[which, half, d - 1],
-            dst_ref=part_in.at[which, to_half, d - 1],
-            send_sem=part_send.at[which, half, d - 1],
-            recv_sem=part_recv.at[which, to_half, d - 1],
+            src_ref=part_out.at[half, d - 1],
+            dst_ref=part_in.at[to_half, d - 1],
+            send_sem=part_send.at[half, d - 1],
+            recv_sem=part_recv.at[to_half, d - 1],
             device_id={"ctx": target},
             device_id_type=MESH,
         )
 
-    def part_routes(which, half, act):
+    def part_routes(half, act):
         for d in range(1, reach + 1):
             up = me + d
             fold = last - up
@@ -206,85 +200,105 @@
 
                 @pl.when(me >= d)
                 def _():
-                    act(part_copy(which, 0, d, me - d, 0))
+                    act(part_copy(0, d, me - d, 0))
 
             else:
 
                 @pl.when(up < n)
                 def _():
-                    act(part_copy(which, 1, d, up, 1))
+                    act(part_copy(1, d, up, 1))
 
                 @pl.when((up >= n) & (fold > me))
                 def _():
-                    act(part_copy(which, 1, d, fold, 0))
-
-    def give_back(which, half, parts):
-        part_out[which, half] = parts.astype(jnp.bfloat16).reshape(reach, st, HEAD_DIM)
+                    act(part_copy(1, d, fold, 0))
+
+    def give_back(half):
         for d in range(1, reach + 1):
             if half == 0:
                 twin = last - 2 * me + d
 
                 @pl.when(twin <= reach)
                 def _():
-                    both = part_out[which, 0, d - 1].astype(jnp.float32)
-                    both += part_out[which, 1, twin - 1].astype(jnp.float32)
-                    part_out[which, 0, d - 1] = both.astype(jnp.bfloat16)
+                    both = part_out[0, d - 1].astype(jnp.float32)
+                    both += part_out[1, twin - 1].astype(jnp.float32)
+                    part_out[0, d - 1] = both.astype(jnp.bfloat16)
 
             else:
 
                 @pl.when(last - me - d == me)
                 def _():
-                    part_in[which, 0, d - 1] = part_out[which, 1, d - 1]
-
-        part_routes(which, half, lambda copy: copy.start())
-
-    kv_arrive(0)
+                    part_in[0, d - 1] = part_out[1, d - 1]
+
+        part_routes(half, lambda copy: copy.start())
+
+    kv_arrive(1)
+    crosses = last - 2 * me <= reach
+
+    @pl.when(crosses)
+    def _():
+        kv_arrive(0)
+
+    for d in range(1, reach + 1):
+        source = last - me - d
+
+        @pl.when(source <= me)
+        def _():
+            k_buf[1, d] = k_buf[0, me - source]
+            v_buf[1, d] = v_buf[0, me - source]
+
     factor = scaling * math.log2(math.e)
     for half in (1, 0):
+        if half == 0:
+
+            @pl.when(jnp.logical_not(crosses))
+            def _():
+                kv_arrive(0)
+
+        k_rest = k_buf[half, 1:].reshape(reach * st, HEAD_DIM)
+        v_rest = v_buf[half, 1:].reshape(reach * st, HEAD_DIM)
         for h in range(0, heads, PAIR):
             cols = slice(h * HEAD_DIM, h * HEAD_DIM + wide)
-            q_cols = gather(q_buf, half, h, PAIR)
-            far = dot(k_buf[half, reach], q_cols, NT)
-            scores = [jnp.where(lower_wide, s_own[half, :, cols], far)]
-            scores += [dot(k_buf[half, d], q_cols, NT) for d in range(1, reach)]
+
+            def blocks(own, rest):
+                merged = jnp.where(lower_wide, own[half, :, cols], rest[(reach - 1) * st :])
+                return [merged] + [rest[(d - 1) * st : d * st] for d in range(1, reach)]
+
+            scores = blocks(s_own, dot(k_rest, gather(q_buf, half, h, PAIR), NT))
             scores = [score + mask for score, mask in zip(scores, bias[half])]
             top = functools.reduce(jnp.maximum, scores)
             top = jnp.max(top, axis=0, keepdims=True)
             weights = [jnp.exp2((score - top) * factor) for score in scores]
             total = jnp.sum(functools.reduce(jnp.add, weights), axis=0, keepdims=True)
             inverse = 1.0 / total
-            for d in range(reach):
-                weight = weights[d] * inverse
-                w_buf[half, d, :, cols] = weight
-                low = weight.astype(jnp.bfloat16)
-                if d == 0:
-                    low_own = low * lower_low
-                    p_buf[half, :st, cols] = low_own
-                    p_buf[half, reach * st :, cols] = low - low_own
-                else:
-                    p_buf[half, d * st : (d + 1) * st, cols] = low
-        give_back(1, half, matmul(p_buf[half, st:], gather(g_buf, half, 0, heads)))
-
-    kv_arrive(1)
-    for half in (1, 0):
-        for h in range(0, heads, PAIR):
-            cols = slice(h * HEAD_DIM, h * HEAD_DIM + wide)
-            g_cols = gather(g_buf, half, h, PAIR)
-            far = dot(v_buf[half, reach], g_cols, NT)
-            grads = [jnp.where(lower_wide, w_own[half, :, cols], far)]
-            grads += [dot(v_buf[half, d], g_cols, NT) for d in range(1, reach)]
-            weights = [w_buf[half, d, :, cols] for d in range(reach)]
+            weights = [weight * inverse for weight in weights]
+            grads = blocks(w_own, dot(v_rest, gather(g_buf, half, h, PAIR), NT))
             delta = functools.reduce(jnp.add, [w * g for w, g in zip(weights, grads)])
             delta = jnp.sum(delta, axis=0, keepdims=True)
             for d in range(reach):
+                low = weights[d].astype(jnp.bfloat16)
                 slope = (weights[d] * (grads[d] - delta)).astype(jnp.bfloat16)
                 if d == 0:
+                    low_own = low * lower_low
                     slope_own = slope * lower_low
+                    p_buf[half, :st, cols] = low_own
                     d_buf[half, :st, cols] = slope_own
+                    p_buf[half, reach * st :, cols] = low - low_own
                     d_buf[half, reach * st :, cols] = slope - slope_own
                 else:
+                    p_buf[half, d * st : (d + 1) * st, cols] = low
                     d_buf[half, d * st : (d + 1) * st, cols] = slope
-        give_back(0, half, matmul(d_buf[half, st:], gather(q_buf, half, 0, heads)) * scaling)
+
+        part_out[half, :, :st] = (
+            (matmul(d_buf[half, st:], gather(q_buf, half, 0, heads)) * scaling)
+            .astype(jnp.bfloat16)
+            .reshape(reach, st, HEAD_DIM)
+        )
+        part_out[half, :, st:] = (
+            matmul(p_buf[half, st:], gather(g_buf, half, 0, heads))
+            .astype(jnp.bfloat16)
+            .reshape(reach, st, HEAD_DIM)
+        )
+        give_back(half)
 
     for half in (1, 0):
         k_turn = jnp.concatenate([k_buf[half, d].T for d in range(reach + 1)], axis=1)
@@ -299,26 +313,25 @@
                 att_ref[rows[half], out] = att[:, own].T.astype(jnp.bfloat16)
                 dq_ref[rows[half], out] = grad[:, own].T.astype(jnp.bfloat16)
 
-    for which, half in ((1, 1), (1, 0), (0, 1), (0, 0)):
-        if which == 0:
-            own = matmul(d_buf[half, :st], gather(q_buf, half, 0, heads)) * scaling
-        else:
-            own = matmul(p_buf[half, :st], gather(g_buf, half, 0, heads))
+    for half in (1, 0):
+        key_own = matmul(d_buf[half, :st], gather(q_buf, half, 0, heads)) * scaling
+        value_own = matmul(p_buf[half, :st], gather(g_buf, half, 0, heads))
         for d in range(1, reach + 1):
             arrives = ((me + d < n) | (last - me - d < me)) if half == 0 else (me >= d)
 
             @pl.when(arrives)
             def _():
-                part_copy(which, half, d, me, half).wait_recv()
+                part_copy(half, d, me, half).wait_recv()
 
         for d in range(reach):
-            own += part_in[which, half, d].astype(jnp.float32)
-        (dk_ref, dv_ref)[which][rows[half]] = own.astype(jnp.bfloat16)
-
-    for which in range(2):
-        kv_routes(which, lambda copy: copy.wait_send())
-        for half in range(2):
-            part_routes(which, half, lambda copy: copy.wait_send())
+            key_own += part_in[half, d, :st].astype(jnp.float32)
+            value_own += part_in[half, d, st:].astype(jnp.float32)
+        dk_ref[rows[half]] = key_own.astype(jnp.bfloat16)
+        dv_ref[rows[half]] = value_own.astype(jnp.bfloat16)
+
+    for half in (1, 0):
+        kv_routes(half, lambda copy: copy.wait_send())
+        part_routes(half, lambda copy: copy.wait_send())
 
 
 def write_out(*refs):
@@ -356,17 +369,16 @@
             pltpu.VMEM((2, reach + 1, st, HEAD_DIM), low),
             pltpu.VMEM((2, st, width), jnp.float32),
             pltpu.VMEM((2, st, width), jnp.float32),
-            pltpu.VMEM((2, reach, st, width), jnp.float32),
             pltpu.VMEM((2, (reach + 1) * st, width), low),
             pltpu.VMEM((2, (reach + 1) * st, width), low),
-            pltpu.VMEM((2, 2, reach, st, HEAD_DIM), low),
-            pltpu.VMEM((2, 2, reach, st, HEAD_DIM), low),
+            pltpu.VMEM((2, reach, 2 * st, HEAD_DIM), low),
+            pltpu.VMEM((2, reach, 2 * st, HEAD_DIM), low),
             pltpu.SemaphoreType.DMA,
             pltpu.SemaphoreType.DMA((2, 4)),
             pltpu.SemaphoreType.DMA((2, reach, 2)),
             pltpu.SemaphoreType.DMA((2, reach, 2)),
-            pltpu.SemaphoreType.DMA((2, 2, reach)),
-            pltpu.SemaphoreType.DMA((2, 2, reach)),
+            pltpu.SemaphoreType.DMA((2, reach)),
+            pltpu.SemaphoreType.DMA((2, reach)),
         ],
         compiler_params=pltpu.CompilerParams(
             collective_id=0, has_side_effects=True, vmem_limit_bytes=40 * 1024 * 1024

time: 17 us -> 17.8 us (1.047)
  Pallas kernels: 16.2 us -> 17 us
    pallas_call x1, Pallas kernels: 15.1 us -> 16 us  [shards(): pl.pallas_call(functools.partial(kernel, n, reach, heads), out_shape=shap...]
where the time goes in v4:
time: 17.8 us; the launch traced here: 17.7 us
  Pallas kernels  17 us (96%)
  between operations  0.64 us (4%)
    pallas_call x1, Pallas kernels, shards(): pl.pallas_call(functools.partial(kernel, n, reach, heads), out_shape=shap...  16 us
    pallas_call x1, Pallas kernels, shards(): pl.pallas_call(write_out, out_shape=shapes, in_specs=[anywhere] * 4, out_...  1.03 us

profile of v4, /device:TPU:0, one launch (start us, length us, event | category | flops | bytes accessed | tf_op | source)
XLA Modules:
  0.0 17.7 jit_solution(16974461645272495441)
XLA Ops:
  0.6 16.0 %shard_map.84 = (bf16[256,1024]{1,0:T(8,128)(2,1)S(1)}, bf16[256,1024]{1,0:T(8,128)(2,1)S(1)}, bf16[256,128]{1,0:T(8,128)(2,1)S(1)}, bf16[256,128]{1,0:T(8,128)(2,1)S(1)}) custom-call(s32[16]{0:T(128)} %docs_hbm.1, bf16[256,1024]{1,0:T(8,128)(2,1)} %q_hbm.1, bf16[256,128]{1,0:T(8,128)(2,1)} %k_hbm.1, bf16[256,128]{1,0:T(8,128)(2,1)} %v_hbm.1, ...), custom_call_target="tpu_custom_call" | custom-call | flops 1207959552 | bytes 2359296 | tf_op jit(solution)/shard_map/pallas_call | solution.py:359
  16.6 1.0 %shard_map.85 = (bf16[256,1024]{1,0:T(8,128)(2,1)}, bf16[256,1024]{1,0:T(8,128)(2,1)}, bf16[256,128]{1,0:T(8,128)(2,1)}, bf16[256,128]{1,0:T(8,128)(2,1)}) custom-call(bf16[256,1024]{1,0:T(8,128)(2,1)S(1)} %get-tuple-element.8.refs_0_, bf16[256,1024]{1,0:T(8,128)(2,1)S(1)} %get-tuple-element.9.refs_1_, bf16[256,128]{1,0:T(8,128)(2,1)S(1)} %get-tuple-element.10.refs_2_, ...), custom_call_target="tpu_custom_call" | custom-call | tf_op jit(solution)/shard_map/pallas_call | solution.py:395

commit v5 on v3

--- a/solution.py
+++ b/solution.py
@@ -97,6 +97,58 @@
         def _():
             part_in[:, 0, d - 1] = jnp.zeros_like(part_in[:, 0, d - 1])
 
+    pl.semaphore_wait(barrier, jnp.minimum(me, reach) + jnp.minimum(n - 1 - me, reach))
+
+    def kv_copy(which, half, d, target, to_half):
+        src, dst = ((k_hbm, k_buf), (v_hbm, v_buf))[which]
+        return pltpu.make_async_remote_copy(
+            src_ref=src.at[rows[half]],
+            dst_ref=dst.at[to_half, d],
+            send_sem=kv_send.at[half, d - 1, which],
+            recv_sem=kv_recv.at[to_half, d - 1, which],
+            device_id={"ctx": target},
+            device_id_type=MESH,
+        )
+
+    def kv_routes(which, act):
+        for d in range(1, reach + 1):
+            up = me + d
+            fold = last - up
+
+            @pl.when(me >= d)
+            def _():
+                act(kv_copy(which, 1, d, me - d, 1))
+
+            @pl.when(up < n)
+            def _():
+                act(kv_copy(which, 0, d, up, 0))
+
+            @pl.when((up >= n) & (fold < me))
+            def _():
+                act(kv_copy(which, 0, d, fold, 1))
+
+    def kv_arrive(which):
+        buf = (k_buf, v_buf)[which]
+        for d in range(1, reach + 1):
+
+            @pl.when(me >= d)
+            def _():
+                kv_copy(which, 0, d, me, 0).wait_recv()
+
+        for d in range(1, reach + 1):
+            source = last - me - d
+
+            @pl.when(source > me)
+            def _():
+                kv_copy(which, 1, d, me, 1).wait_recv()
+
+            @pl.when(source <= me)
+            def _():
+                buf[1, d] = buf[0, me - source]
+
+    kv_routes(0, lambda copy: copy.start())
+    kv_routes(1, lambda copy: copy.start())
+
     docs_copy.wait()
 
     lane = lax.broadcasted_iota(jnp.int32, (st, st), 1)
@@ -121,58 +173,6 @@
         blocks = [jnp.where(block >= first, 0.0, -1e30) for block in blocks]
         bias.append([jnp.concatenate([block] * PAIR, axis=1) for block in blocks])
 
-    pl.semaphore_wait(barrier, jnp.minimum(me, reach) + jnp.minimum(n - 1 - me, reach))
-
-    def kv_copy(which, half, d, target, to_half):
-        src, dst = ((k_hbm, k_buf), (v_hbm, v_buf))[which]
-        return pltpu.make_async_remote_copy(
-            src_ref=src.at[rows[half]],
-            dst_ref=dst.at[to_half, d],
-            send_sem=kv_send.at[half, d - 1, which],
-            recv_sem=kv_recv.at[to_half, d - 1, which],
-            device_id={"ctx": target},
-            device_id_type=MESH,
-        )
-
-    def kv_routes(which, act):
-        for d in range(1, reach + 1):
-            up = me + d
-            fold = last - up
-
-            @pl.when(me >= d)
-            def _():
-                act(kv_copy(which, 1, d, me - d, 1))
-
-            @pl.when(up < n)
-            def _():
-                act(kv_copy(which, 0, d, up, 0))
-
-            @pl.when((up >= n) & (fold < me))
-            def _():
-                act(kv_copy(which, 0, d, fold, 1))
-
-    def kv_arrive(which):
-        buf = (k_buf, v_buf)[which]
-        for d in range(1, reach + 1):
-
-            @pl.when(me >= d)
-            def _():
-                kv_copy(which, 0, d, me, 0).wait_recv()
-
-        for d in range(1, reach + 1):
-            source = last - me - d
-
-            @pl.when(source > me)
-            def _():
-                kv_copy(which, 1, d, me, 1).wait_recv()
-
-            @pl.when(source <= me)
-            def _():
-                buf[1, d] = buf[0, me - source]
-
-    kv_routes(0, lambda copy: copy.start())
-    kv_routes(1, lambda copy: copy.start())
-
     def gather(buf, half, first, count):
         cols = [
             buf[half, :, h * HEAD_DIM : (h + 1) * HEAD_DIM] for h in range(first, first + count)
@@ -238,15 +238,18 @@
 
         part_routes(which, half, lambda copy: copy.start())
 
+    def blocks(own, others):
+        merged = jnp.where(lower_wide, own, others[(reach - 1) * st :])
+        return [merged] + [others[(d - 1) * st : d * st] for d in range(1, reach)]
+
     kv_arrive(0)
     factor = scaling * math.log2(math.e)
     for half in (1, 0):
+        rest = k_buf[half, 1:].reshape(reach * st, HEAD_DIM)
         for h in range(0, heads, PAIR):
             cols = slice(h * HEAD_DIM, h * HEAD_DIM + wide)
             q_cols = gather(q_buf, half, h, PAIR)
-            far = dot(k_buf[half, reach], q_cols, NT)
-            scores = [jnp.where(lower_wide, s_own[half, :, cols], far)]
-            scores += [dot(k_buf[half, d], q_cols, NT) for d in range(1, reach)]
+            scores = blocks(s_own[half, :, cols], dot(rest, q_cols, NT))
             scores = [score + mask for score, mask in zip(scores, bias[half])]
             top = functools.reduce(jnp.maximum, scores)
             top = jnp.max(top, axis=0, keepdims=True)
@@ -267,12 +270,11 @@
 
     kv_arrive(1)
     for half in (1, 0):
+        rest = v_buf[half, 1:].reshape(reach * st, HEAD_DIM)
         for h in range(0, heads, PAIR):
             cols = slice(h * HEAD_DIM, h * HEAD_DIM + wide)
             g_cols = gather(g_buf, half, h, PAIR)
-            far = dot(v_buf[half, reach], g_cols, NT)
-            grads = [jnp.where(lower_wide, w_own[half, :, cols], far)]
-            grads += [dot(v_buf[half, d], g_cols, NT) for d in range(1, reach)]
+            grads = blocks(w_own[half, :, cols], dot(rest, g_cols, NT))
             weights = [w_buf[half, d, :, cols] for d in range(reach)]
             delta = functools.reduce(jnp.add, [w * g for w, g in zip(weights, grads)])
             delta = jnp.sum(delta, axis=0, keepdims=True)

time: 17 us -> 17.1 us (level)
  no operation moved by 1% of the time
where the time goes in v5:
time: 17.1 us; the launch traced here: 16.9 us
  Pallas kernels  16.3 us (95%)
  between operations  0.64 us (4%)
    pallas_call x1, Pallas kernels, shards(): pl.pallas_call(functools.partial(kernel, n, reach, heads), out_shape=shap...  15.2 us
    pallas_call x1, Pallas kernels, shards(): pl.pallas_call(write_out, out_shape=shapes, in_specs=[anywhere] * 4, out_...  1.03 us

profile of v5, /device:TPU:0, one launch (start us, length us, event | category | flops | bytes accessed | tf_op | source)
XLA Modules:
  0.0 16.9 jit_solution(990056249726164790)
XLA Ops:
  0.6 15.2 %shard_map.84 = (bf16[256,1024]{1,0:T(8,128)(2,1)S(1)}, bf16[256,1024]{1,0:T(8,128)(2,1)S(1)}, bf16[256,128]{1,0:T(8,128)(2,1)S(1)}, bf16[256,128]{1,0:T(8,128)(2,1)S(1)}) custom-call(s32[16]{0:T(128)} %docs_hbm.1, bf16[256,1024]{1,0:T(8,128)(2,1)} %q_hbm.1, bf16[256,128]{1,0:T(8,128)(2,1)} %k_hbm.1, bf16[256,128]{1,0:T(8,128)(2,1)} %v_hbm.1, ...), custom_call_target="tpu_custom_call" | custom-call | flops 1207959552 | bytes 2359296 | tf_op jit(solution)/shard_map/pallas_call | solution.py:348
  15.9 1.0 %shard_map.85 = (bf16[256,1024]{1,0:T(8,128)(2,1)}, bf16[256,1024]{1,0:T(8,128)(2,1)}, bf16[256,128]{1,0:T(8,128)(2,1)}, bf16[256,128]{1,0:T(8,128)(2,1)}) custom-call(bf16[256,1024]{1,0:T(8,128)(2,1)S(1)} %get-tuple-element.8.refs_0_, bf16[256,1024]{1,0:T(8,128)(2,1)S(1)} %get-tuple-element.9.refs_1_, bf16[256,128]{1,0:T(8,128)(2,1)S(1)} %get-tuple-element.10.refs_2_, ...), custom_call_target="tpu_custom_call" | custom-call | tf_op jit(solution)/shard_map/pallas_call | solution.py:385

commit v6 on v4

--- a/solution.py
+++ b/solution.py
@@ -92,9 +92,54 @@
             v_buf[0, d] = jnp.zeros_like(v_buf[0, d])
             part_in[1, d - 1] = jnp.zeros_like(part_in[1, d - 1])
 
-        @pl.when((me + d >= n) & (last - me - d > me))
+        @pl.when((me + d < n) & (last - 2 * me - d <= reach))
         def _():
             part_in[0, d - 1] = jnp.zeros_like(part_in[0, d - 1])
+
+    pl.semaphore_wait(barrier, jnp.minimum(me, reach) + jnp.minimum(n - 1 - me, reach))
+
+    def kv_copy(which, half, d, target, to_half):
+        src, dst = ((k_hbm, k_buf), (v_hbm, v_buf))[which]
+        return pltpu.make_async_remote_copy(
+            src_ref=src.at[rows[half]],
+            dst_ref=dst.at[to_half, d],
+            send_sem=kv_send.at[half, d - 1, which],
+            recv_sem=kv_recv.at[to_half, d - 1, which],
+            device_id={"ctx": target},
+            device_id_type=MESH,
+        )
+
+    def kv_routes(act):
+        for d in range(1, reach + 1):
+            up = me + d
+            fold = last - up
+
+            @pl.when(up < n)
+            def _():
+                for which in range(2):
+                    act(kv_copy(which, 0, d, up, 0))
+
+            @pl.when((up >= n) & (fold < me))
+            def _():
+                for which in range(2):
+                    act(kv_copy(which, 0, d, fold, 1))
+
+            @pl.when(me >= d)
+            def _():
+                for which in range(2):
+                    act(kv_copy(which, 1, d, me - d, 1))
+
+    def kv_arrive(half):
+        for d in range(1, reach + 1):
+            source = last - me - d
+            for which in range(2):
+                arrives = (me >= d) if half == 0 else (source > me)
+
+                @pl.when(arrives)
+                def _():
+                    kv_copy(which, half, d, me, half).wait_recv()
+
+    kv_routes(lambda copy: copy.start())
 
     docs_copy.wait()
 
@@ -120,53 +165,6 @@
         blocks = [jnp.where(block >= first, 0.0, -1e30) for block in blocks]
         bias.append([jnp.concatenate([block] * PAIR, axis=1) for block in blocks])
 
-    pl.semaphore_wait(barrier, jnp.minimum(me, reach) + jnp.minimum(n - 1 - me, reach))
-
-    def kv_copy(which, half, d, target, to_half):
-        src, dst = ((k_hbm, k_buf), (v_hbm, v_buf))[which]
-        return pltpu.make_async_remote_copy(
-            src_ref=src.at[rows[half]],
-            dst_ref=dst.at[to_half, d],
-            send_sem=kv_send.at[half, d - 1, which],
-            recv_sem=kv_recv.at[to_half, d - 1, which],
-            device_id={"ctx": target},
-            device_id_type=MESH,
-        )
-
-    def kv_routes(half, act):
-        for d in range(1, reach + 1):
-            up = me + d
-            fold = last - up
-            for which in range(2):
-                if half == 1:
-
-                    @pl.when(me >= d)
-                    def _():
-                        act(kv_copy(which, 1, d, me - d, 1))
-
-                else:
-
-                    @pl.when(up < n)
-                    def _():
-                        act(kv_copy(which, 0, d, up, 0))
-
-                    @pl.when((up >= n) & (fold < me))
-                    def _():
-                        act(kv_copy(which, 0, d, fold, 1))
-
-    def kv_arrive(half):
-        for d in range(1, reach + 1):
-            source = last - me - d
-            for which in range(2):
-                arrives = (me >= d) if half == 0 else (source > me)
-
-                @pl.when(arrives)
-                def _():
-                    kv_copy(which, half, d, me, half).wait_recv()
-
-    for half in (1, 0):
-        kv_routes(half, lambda copy: copy.start())
-
     def gather(buf, half, first, count):
         cols = [
             buf[half, :, h * HEAD_DIM : (h + 1) * HEAD_DIM] for h in range(first, first + count)
@@ -176,7 +174,7 @@
     for copy in loads:
         copy.wait()
 
-    for half in (1, 0):
+    for half in (0, 1):
         for h in range(0, heads, PAIR):
             cols = slice(h * HEAD_DIM, h * HEAD_DIM + wide)
             s_own[half, :, cols] = dot(k_buf[half, 0], gather(q_buf, half, h, PAIR), NT)
@@ -198,7 +196,7 @@
             fold = last - up
             if half == 0:
 
-                @pl.when(me >= d)
+                @pl.when((me >= d) & (last - 2 * me + d > reach))
                 def _():
                     act(part_copy(0, d, me - d, 0))
 
@@ -208,51 +206,38 @@
                 def _():
                     act(part_copy(1, d, up, 1))
 
-                @pl.when((up >= n) & (fold > me))
+                @pl.when((up >= n) & (fold != me))
                 def _():
                     act(part_copy(1, d, fold, 0))
 
     def give_back(half):
-        for d in range(1, reach + 1):
-            if half == 0:
-                twin = last - 2 * me + d
-
-                @pl.when(twin <= reach)
-                def _():
-                    both = part_out[0, d - 1].astype(jnp.float32)
-                    both += part_out[1, twin - 1].astype(jnp.float32)
-                    part_out[0, d - 1] = both.astype(jnp.bfloat16)
-
-            else:
-
-                @pl.when(last - me - d == me)
+        if half == 1:
+            for d in range(1, reach + 1):
+                fold = last - me - d
+
+                @pl.when(fold < me)
+                def _():
+                    both = part_out[1, d - 1].astype(jnp.float32)
+                    both += part_out[0, me - fold - 1].astype(jnp.float32)
+                    part_out[1, d - 1] = both.astype(jnp.bfloat16)
+
+                @pl.when(fold == me)
                 def _():
                     part_in[0, d - 1] = part_out[1, d - 1]
 
         part_routes(half, lambda copy: copy.start())
 
-    kv_arrive(1)
-    crosses = last - 2 * me <= reach
-
-    @pl.when(crosses)
-    def _():
-        kv_arrive(0)
-
-    for d in range(1, reach + 1):
-        source = last - me - d
-
-        @pl.when(source <= me)
-        def _():
-            k_buf[1, d] = k_buf[0, me - source]
-            v_buf[1, d] = v_buf[0, me - source]
-
     factor = scaling * math.log2(math.e)
-    for half in (1, 0):
-        if half == 0:
-
-            @pl.when(jnp.logical_not(crosses))
-            def _():
-                kv_arrive(0)
+    for half in (0, 1):
+        kv_arrive(half)
+        if half == 1:
+            for d in range(1, reach + 1):
+                source = last - me - d
+
+                @pl.when(source <= me)
+                def _():
+                    k_buf[1, d] = k_buf[0, me - source]
+                    v_buf[1, d] = v_buf[0, me - source]
 
         k_rest = k_buf[half, 1:].reshape(reach * st, HEAD_DIM)
         v_rest = v_buf[half, 1:].reshape(reach * st, HEAD_DIM)
@@ -300,7 +285,7 @@
         )
         give_back(half)
 
-    for half in (1, 0):
+    for half in (0, 1):
         k_turn = jnp.concatenate([k_buf[half, d].T for d in range(reach + 1)], axis=1)
         v_turn = jnp.concatenate([v_buf[half, d].T for d in range(reach + 1)], axis=1)
         for h in range(0, heads, PAIR):
@@ -313,11 +298,14 @@
                 att_ref[rows[half], out] = att[:, own].T.astype(jnp.bfloat16)
                 dq_ref[rows[half], out] = grad[:, own].T.astype(jnp.bfloat16)
 
-    for half in (1, 0):
+    for half in (0, 1):
         key_own = matmul(d_buf[half, :st], gather(q_buf, half, 0, heads)) * scaling
         value_own = matmul(p_buf[half, :st], gather(g_buf, half, 0, heads))
         for d in range(1, reach + 1):
-            arrives = ((me + d < n) | (last - me - d < me)) if half == 0 else (me >= d)
+            arrives = me >= d
+            if half == 0:
+                joined = (me + d < n) & (last - 2 * me - d <= reach)
+                arrives = jnp.logical_not(joined) & (last - me - d != me)
 
             @pl.when(arrives)
             def _():
@@ -329,8 +317,8 @@
         dk_ref[rows[half]] = key_own.astype(jnp.bfloat16)
         dv_ref[rows[half]] = value_own.astype(jnp.bfloat16)
 
-    for half in (1, 0):
-        kv_routes(half, lambda copy: copy.wait_send())
+    kv_routes(lambda copy: copy.wait_send())
+    for half in (0, 1):
         part_routes(half, lambda copy: copy.wait_send())
 
 

time: 17.8 us -> 15.8 us (0.89)
  Pallas kernels: 17 us -> 15 us
    pallas_call x1, Pallas kernels: 16 us -> 13.9 us  [shards(): pl.pallas_call(functools.partial(kernel, n, reach, heads), out_shape=shap...]
where the time goes in v6:
time: 15.8 us; the launch traced here: 15.6 us
  Pallas kernels  15 us (95%)
  between operations  0.64 us (4%)
    pallas_call x1, Pallas kernels, shards(): pl.pallas_call(functools.partial(kernel, n, reach, heads), out_shape=shap...  13.9 us
    pallas_call x1, Pallas kernels, shards(): pl.pallas_call(write_out, out_shape=shapes, in_specs=[anywhere] * 4, out_...  1.03 us

profile of v6, /device:TPU:0, one launch (start us, length us, event | category | flops | bytes accessed | tf_op | source)
XLA Modules:
  0.0 15.6 jit_solution(6925137050537027864)
XLA Ops:
  0.6 13.9 %shard_map.84 = (bf16[256,1024]{1,0:T(8,128)(2,1)S(1)}, bf16[256,1024]{1,0:T(8,128)(2,1)S(1)}, bf16[256,128]{1,0:T(8,128)(2,1)S(1)}, bf16[256,128]{1,0:T(8,128)(2,1)S(1)}) custom-call(s32[16]{0:T(128)} %docs_hbm.1, bf16[256,1024]{1,0:T(8,128)(2,1)} %q_hbm.1, bf16[256,128]{1,0:T(8,128)(2,1)} %k_hbm.1, bf16[256,128]{1,0:T(8,128)(2,1)} %v_hbm.1, ...), custom_call_target="tpu_custom_call" | custom-call | flops 1207959552 | bytes 2359296 | tf_op jit(solution)/shard_map/pallas_call | solution.py:347
  14.6 1.0 %shard_map.85 = (bf16[256,1024]{1,0:T(8,128)(2,1)}, bf16[256,1024]{1,0:T(8,128)(2,1)}, bf16[256,128]{1,0:T(8,128)(2,1)}, bf16[256,128]{1,0:T(8,128)(2,1)}) custom-call(bf16[256,1024]{1,0:T(8,128)(2,1)S(1)} %get-tuple-element.8.refs_0_, bf16[256,1024]{1,0:T(8,128)(2,1)S(1)} %get-tuple-element.9.refs_1_, bf16[256,128]{1,0:T(8,128)(2,1)S(1)} %get-tuple-element.10.refs_2_, ...), custom_call_target="tpu_custom_call" | custom-call | tf_op jit(solution)/shard_map/pallas_call | solution.py:383

commit v7 on v6

--- a/solution.py
+++ b/solution.py
@@ -109,25 +109,28 @@
             device_id_type=MESH,
         )
 
-    def kv_routes(act):
+    def kv_routes(to_half, act):
         for d in range(1, reach + 1):
             up = me + d
             fold = last - up
-
-            @pl.when(up < n)
-            def _():
-                for which in range(2):
-                    act(kv_copy(which, 0, d, up, 0))
-
-            @pl.when((up >= n) & (fold < me))
-            def _():
-                for which in range(2):
-                    act(kv_copy(which, 0, d, fold, 1))
-
-            @pl.when(me >= d)
-            def _():
-                for which in range(2):
-                    act(kv_copy(which, 1, d, me - d, 1))
+            if to_half == 0:
+
+                @pl.when(up < n)
+                def _():
+                    for which in range(2):
+                        act(kv_copy(which, 0, d, up, 0))
+
+            else:
+
+                @pl.when((up >= n) & (fold < me))
+                def _():
+                    for which in range(2):
+                        act(kv_copy(which, 0, d, fold, 1))
+
+                @pl.when(me >= d)
+                def _():
+                    for which in range(2):
+                        act(kv_copy(which, 1, d, me - d, 1))
 
     def kv_arrive(half):
         for d in range(1, reach + 1):
@@ -139,7 +142,7 @@
                 def _():
                     kv_copy(which, half, d, me, half).wait_recv()
 
-    kv_routes(lambda copy: copy.start())
+    kv_routes(0, lambda copy: copy.start())
 
     docs_copy.wait()
 
@@ -171,10 +174,11 @@
         ]
         return jnp.concatenate(cols, axis=0)
 
-    for copy in loads:
-        copy.wait()
-
     for half in (0, 1):
+        for copy in loads[4 * half : 4 * half + 4]:
+            copy.wait()
+        if half == 1:
+            kv_routes(1, lambda copy: copy.start())
         for h in range(0, heads, PAIR):
             cols = slice(h * HEAD_DIM, h * HEAD_DIM + wide)
             s_own[half, :, cols] = dot(k_buf[half, 0], gather(q_buf, half, h, PAIR), NT)
@@ -317,8 +321,8 @@
         dk_ref[rows[half]] = key_own.astype(jnp.bfloat16)
         dv_ref[rows[half]] = value_own.astype(jnp.bfloat16)
 
-    kv_routes(lambda copy: copy.wait_send())
     for half in (0, 1):
+        kv_routes(half, lambda copy: copy.wait_send())
         part_routes(half, lambda copy: copy.wait_send())
 
 

time: 15.8 us -> 15.8 us (level)
  no operation moved by 1% of the time
where the time goes in v7:
time: 15.8 us; the launch traced here: 15.6 us
  Pallas kernels  15 us (95%)
  between operations  0.64 us (4%)
    pallas_call x1, Pallas kernels, shards(): pl.pallas_call(functools.partial(kernel, n, reach, heads), out_shape=shap...  13.9 us
    pallas_call x1, Pallas kernels, shards(): pl.pallas_call(write_out, out_shape=shapes, in_specs=[anywhere] * 4, out_...  1.03 us

profile of v7, /device:TPU:0, one launch (start us, length us, event | category | flops | bytes accessed | tf_op | source)
XLA Modules:
  0.0 15.6 jit_solution(11310536364427078640)
XLA Ops:
  0.6 13.9 %shard_map.84 = (bf16[256,1024]{1,0:T(8,128)(2,1)S(1)}, bf16[256,1024]{1,0:T(8,128)(2,1)S(1)}, bf16[256,128]{1,0:T(8,128)(2,1)S(1)}, bf16[256,128]{1,0:T(8,128)(2,1)S(1)}) custom-call(s32[16]{0:T(128)} %docs_hbm.1, bf16[256,1024]{1,0:T(8,128)(2,1)} %q_hbm.1, bf16[256,128]{1,0:T(8,128)(2,1)} %k_hbm.1, bf16[256,128]{1,0:T(8,128)(2,1)} %v_hbm.1, ...), custom_call_target="tpu_custom_call" | custom-call | flops 1207959552 | bytes 2359296 | tf_op jit(solution)/shard_map/pallas_call | solution.py:351
  14.6 1.0 %shard_map.85 = (bf16[256,1024]{1,0:T(8,128)(2,1)}, bf16[256,1024]{1,0:T(8,128)(2,1)}, bf16[256,128]{1,0:T(8,128)(2,1)}, bf16[256,128]{1,0:T(8,128)(2,1)}) custom-call(bf16[256,1024]{1,0:T(8,128)(2,1)S(1)} %get-tuple-element.8.refs_0_, bf16[256,1024]{1,0:T(8,128)(2,1)S(1)} %get-tuple-element.9.refs_1_, bf16[256,128]{1,0:T(8,128)(2,1)S(1)} %get-tuple-element.10.refs_2_, ...), custom_call_target="tpu_custom_call" | custom-call | tf_op jit(solution)/shard_map/pallas_call | solution.py:387

commit v8 on v6

--- a/solution.py
+++ b/solution.py
@@ -12,7 +12,6 @@
 DOC_STRETCHES = 8
 PAIR = 2
 MESH = pl.DeviceIdType.MESH
-NT = (((1,), (1,)), ((), ()))
 
 
 def kernel(
@@ -31,6 +30,8 @@
     docs_ref,
     q_buf,
     g_buf,
+    q_turn,
+    g_turn,
     k_buf,
     v_buf,
     s_own,
@@ -177,8 +178,12 @@
     for half in (0, 1):
         for h in range(0, heads, PAIR):
             cols = slice(h * HEAD_DIM, h * HEAD_DIM + wide)
-            s_own[half, :, cols] = dot(k_buf[half, 0], gather(q_buf, half, h, PAIR), NT)
-            w_own[half, :, cols] = dot(v_buf[half, 0], gather(g_buf, half, h, PAIR), NT)
+            for j in range(h, h + PAIR):
+                own = slice(j * HEAD_DIM, (j + 1) * HEAD_DIM)
+                q_turn[half, :, own] = q_buf[half, :, own].T
+                g_turn[half, :, own] = g_buf[half, :, own].T
+            s_own[half, :, cols] = matmul(k_buf[half, 0], q_turn[half, :, cols])
+            w_own[half, :, cols] = matmul(v_buf[half, 0], g_turn[half, :, cols])
 
     def part_copy(half, d, target, to_half):
         return pltpu.make_async_remote_copy(
@@ -248,7 +253,7 @@
                 merged = jnp.where(lower_wide, own[half, :, cols], rest[(reach - 1) * st :])
                 return [merged] + [rest[(d - 1) * st : d * st] for d in range(1, reach)]
 
-            scores = blocks(s_own, dot(k_rest, gather(q_buf, half, h, PAIR), NT))
+            scores = blocks(s_own, matmul(k_rest, q_turn[half, :, cols]))
             scores = [score + mask for score, mask in zip(scores, bias[half])]
             top = functools.reduce(jnp.maximum, scores)
             top = jnp.max(top, axis=0, keepdims=True)
@@ -256,7 +261,7 @@
             total = jnp.sum(functools.reduce(jnp.add, weights), axis=0, keepdims=True)
             inverse = 1.0 / total
             weights = [weight * inverse for weight in weights]
-            grads = blocks(w_own, dot(v_rest, gather(g_buf, half, h, PAIR), NT))
+            grads = blocks(w_own, matmul(v_rest, g_turn[half, :, cols]))
             delta = functools.reduce(jnp.add, [w * g for w, g in zip(weights, grads)])
             delta = jnp.sum(delta, axis=0, keepdims=True)
             for d in range(reach):
@@ -353,6 +358,8 @@
             pltpu.SMEM(doc_lengths.shape, jnp.int32),
             pltpu.VMEM((2, st, width), low),
             pltpu.VMEM((2, st, width), low),
+            pltpu.VMEM((2, HEAD_DIM, width), low),
+            pltpu.VMEM((2, HEAD_DIM, width), low),
             pltpu.VMEM((2, reach + 1, st, HEAD_DIM), low),
             pltpu.VMEM((2, reach + 1, st, HEAD_DIM), low),
             pltpu.VMEM((2, st, width), jnp.float32),

time: 15.8 us -> 15.7 us (level)
  no operation moved by 1% of the time
where the time goes in v8:
time: 15.7 us; the launch traced here: 15.6 us
  Pallas kernels  15 us (96%)
  between operations  0.64 us (4%)
    pallas_call x1, Pallas kernels, shards(): pl.pallas_call(functools.partial(kernel, n, reach, heads), out_shape=shap...  13.9 us
    pallas_call x1, Pallas kernels, shards(): pl.pallas_call(write_out, out_shape=shapes, in_specs=[anywhere] * 4, out_...  1.03 us

profile of v8, /device:TPU:0, one launch (start us, length us, event | category | flops | bytes accessed | tf_op | source)
XLA Modules:
  0.0 15.6 jit_solution(6804214866329325501)
XLA Ops:
  0.6 13.9 %shard_map.84 = (bf16[256,1024]{1,0:T(8,128)(2,1)S(1)}, bf16[256,1024]{1,0:T(8,128)(2,1)S(1)}, bf16[256,128]{1,0:T(8,128)(2,1)S(1)}, bf16[256,128]{1,0:T(8,128)(2,1)S(1)}) custom-call(s32[16]{0:T(128)} %docs_hbm.1, bf16[256,1024]{1,0:T(8,128)(2,1)} %q_hbm.1, bf16[256,128]{1,0:T(8,128)(2,1)} %k_hbm.1, bf16[256,128]{1,0:T(8,128)(2,1)} %v_hbm.1, ...), custom_call_target="tpu_custom_call" | custom-call | flops 1207959552 | bytes 2359296 | tf_op jit(solution)/shard_map/pallas_call | solution.py:352
  14.6 1.0 %shard_map.85 = (bf16[256,1024]{1,0:T(8,128)(2,1)}, bf16[256,1024]{1,0:T(8,128)(2,1)}, bf16[256,128]{1,0:T(8,128)(2,1)}, bf16[256,128]{1,0:T(8,128)(2,1)}) custom-call(bf16[256,1024]{1,0:T(8,128)(2,1)S(1)} %get-tuple-element.8.refs_0_, bf16[256,1024]{1,0:T(8,128)(2,1)S(1)} %get-tuple-element.9.refs_1_, bf16[256,128]{1,0:T(8,128)(2,1)S(1)} %get-tuple-element.10.refs_2_, ...), custom_call_target="tpu_custom_call" | custom-call | tf_op jit(solution)/shard_map/pallas_call | solution.py:390
